TPU v7x, 128 devices: a whole 4x4x4 slice. The times are simulated.
128 devices in a mesh: group: 16 (over x, z), cuts: 8 (over y, core).
Axes of the slice: x: 4, y: 4, z: 4, core: 2. Of those that a mesh axis runs over, the one named last changes fastest.
Arguments:
- acts: bfloat16 [2048, 6144], P('group', 'cuts'), may hold values from -6 to 6
- grad_out: bfloat16 [2048, 6144], P('group', 'cuts'), may hold values from -6 to 6
- expert_ids: int32 [2048, 2], P('group'), may hold values from 0 to 3, all different within a row; in each aligned block of 128 rows (0 to 127, 128 to 255, ...) at most 80 rows name the same one
- combine: float32 [2048, 2], P('group'), may hold values from 0.1 to 1
- gate_pre: bfloat16 [1280, 65536], P(None, ('group', 'cuts')), may hold values from -6 to 6
- up_weight: bfloat16 [6144, 65536], P(None, ('group', 'cuts')), may hold values from -0.078125 to 0.078125
- down_weight: bfloat16 [65536, 6144], P(('group', 'cuts')), may hold values from -0.046875 to 0.046875
Outputs:
- grad_acts: bfloat16 [2048, 6144], P('group', 'cuts')
- grad_combine: float32 [2048, 2], P('group')
- grad_up: bfloat16 [6144, 65536], P(None, ('group', 'cuts'))
- grad_down: bfloat16 [65536, 6144], P(('group', 'cuts'))
- grad_gate_pre: bfloat16 [1280, 65536], P(None, ('group', 'cuts'))
Inputs may be any that keep to these rules, and one draw needn't show every extreme that they name: `expert_ids`: each token names 2 different experts; in each aligned block of 128 tokens no expert is named by more than 80 tokens, a bound that some block reaches.
All inputs are finite; a program needn't handle non-finite values.
Results may differ from a plain program's by a relative error of at most 0.023.
Values may be sent and summed in bfloat16 or wider, within the bound.
No kernel may reach another device: no remote copies, remote signals or barrier semaphores. Data moves between devices by JAX's collectives and lax.ppermute only.
A program may use at most 192 MiB of HBM per device.

v0:
```python
import math

import jax
import jax.numpy as jnp
from jax import lax
from jax.sharding import PartitionSpec as P

EXPERTS = 4
MOST = 80


root_coef = math.sqrt(2.0 / math.pi)


def gelu_pair(gate):
    inner = root_coef * (gate + 0.044715 * gate * gate * gate)
    tval = jnp.tanh(inner)
    act = 0.5 * gate * (1.0 + tval)
    slope = 0.5 * (1.0 + tval) + 0.5 * gate * (1.0 - tval * tval) * root_coef * (
        1.0 + 3.0 * 0.044715 * gate * gate
    )
    return (act, slope)


def expert_work(slot_acts, slot_grad, slot_weight, gate_slice, up_slice, down_slice):
    upv = jnp.dot(slot_acts, up_slice, preferred_element_type=jnp.float32)
    act, slope = gelu_pair(gate_slice.astype(jnp.float32))
    hidden = (act * upv).astype(jnp.bfloat16)
    raw = lax.dot_general(
        slot_grad, down_slice, (((1,), (1,)), ((), ())), preferred_element_type=jnp.float32
    )
    dhid = slot_weight[:, None] * raw
    dup = (dhid * act).astype(jnp.bfloat16)
    grad_gate = (dhid * upv * slope).astype(jnp.bfloat16)
    wgrad = (slot_weight[:, None] * slot_grad.astype(jnp.float32)).astype(jnp.bfloat16)
    grad_up = lax.dot_general(
        slot_acts, dup, (((0,), (0,)), ((), ())), preferred_element_type=jnp.float32
    ).astype(jnp.bfloat16)
    grad_down = lax.dot_general(
        hidden, wgrad, (((0,), (0,)), ((), ())), preferred_element_type=jnp.float32
    ).astype(jnp.bfloat16)
    slot_input = lax.dot_general(
        dup, up_slice, (((1,), (1,)), ((), ())), preferred_element_type=jnp.float32
    )
    slot_route = jnp.sum(hidden.astype(jnp.float32) * raw, axis=1)
    return (slot_input, slot_route, grad_up, grad_down, grad_gate)


def slot_tables(expert_ids, combine):
    eidx = jnp.arange(EXPERTS, dtype=jnp.int32)
    hit = expert_ids[:, :, None] == eidx
    member = jnp.any(hit, axis=1).astype(jnp.int32)
    wtab = jnp.sum(combine[:, :, None] * hit.astype(jnp.float32), axis=1)
    rank = jnp.cumsum(member, axis=0) - member
    places = jnp.arange(MOST, dtype=jnp.int32)
    match = ((member.T[:, None, :] == 1) & (rank.T[:, None, :] == places[None, :, None])).astype(
        jnp.float32
    )
    slot_weight = jnp.einsum("ept,te->ep", match, wtab, precision=lax.Precision.HIGHEST)
    return (match, slot_weight, hit)


def place_rows(match, rows, copies):
    placed = jnp.einsum(
        "ept,td->epd", match.astype(jnp.bfloat16), rows, preferred_element_type=jnp.float32
    )
    return jnp.repeat(placed.astype(jnp.bfloat16), copies, axis=0)


def back_to_tokens(match, slot_input, slot_route, copies):
    width = slot_input.shape[-1]
    summed = jnp.sum(slot_input.reshape(EXPERTS, copies, MOST, width), axis=1)
    routes = jnp.sum(slot_route.reshape(EXPERTS, copies, MOST), axis=1)
    token_input = jnp.einsum("ept,epd->td", match, summed, precision=lax.Precision.HIGHEST)
    token_route = jnp.einsum("ept,ep->te", match, routes, precision=lax.Precision.HIGHEST)
    return (token_input, token_route)


def body(acts, grad_out, expert_ids, combine, gate_pre, up_weight, down_weight):
    groups = lax.axis_size("group")
    copies = groups // EXPERTS
    match, slot_weight, hit = slot_tables(expert_ids, combine)
    weight_send = jnp.repeat(slot_weight, copies, axis=0)
    full_acts, full_grad = (
        lax.all_gather(acts, "cuts", axis=1, tiled=True),
        lax.all_gather(grad_out, "cuts", axis=1, tiled=True),
    )
    recv_acts, recv_grad, recv_weight = (
        lax.all_to_all(
            place_rows(match, full_acts, copies), "group", split_axis=0, concat_axis=0, tiled=True
        ),
        lax.all_to_all(
            place_rows(match, full_grad, copies), "group", split_axis=0, concat_axis=0, tiled=True
        ),
        lax.all_to_all(
            weight_send.astype(jnp.bfloat16), "group", split_axis=0, concat_axis=0, tiled=True
        ).astype(weight_send.dtype),
    )
    width = full_acts.shape[1]
    slot_input, slot_route, grad_up, grad_down, grad_gate = expert_work(
        recv_acts.reshape(-1, width),
        recv_grad.reshape(-1, width),
        recv_weight.reshape(-1),
        gate_pre,
        up_weight,
        down_weight,
    )
    back_input, back_route = (
        lax.all_to_all(
            slot_input.reshape(groups, MOST, width).astype(jnp.bfloat16),
            "group",
            split_axis=0,
            concat_axis=0,
            tiled=True,
        ).astype(jnp.float32),
        lax.all_to_all(
            slot_route.reshape(groups, MOST).astype(jnp.bfloat16),
            "group",
            split_axis=0,
            concat_axis=0,
            tiled=True,
        ).astype(jnp.float32),
    )
    token_input, token_route = back_to_tokens(match, back_input, back_route, copies)
    own_input = lax.psum_scatter(
        token_input.astype(jnp.bfloat16), "cuts", scatter_dimension=1, tiled=True
    )
    route_terms = jnp.sum(token_route[:, None, :] * hit.astype(jnp.float32), axis=2)
    grad_combine = lax.psum(route_terms, "cuts")
    return (own_input, grad_combine, grad_up, grad_down, grad_gate)


def solution(mesh):
    return jax.shard_map(
        body,
        mesh=mesh,
        in_specs=(
            P("group", "cuts"),
            P("group", "cuts"),
            P("group", None),
            P("group", None),
            P(None, ("group", "cuts")),
            P(None, ("group", "cuts")),
            P(("group", "cuts"), None),
        ),
        out_specs=(
            P("group", "cuts"),
            P("group", None),
            P(None, ("group", "cuts")),
            P(("group", "cuts"), None),
            P(None, ("group", "cuts")),
        ),
        check_vma=False,
    )
```

profile of v0, /device:TPU:0, one launch (start us, length us, event | category | flops | bytes accessed | tf_op | source)
XLA Modules:
  0.0 993.5 jit_solution(5957260314499064263)
XLA Ops:
  7.2 0.0 all-gather.5.cloned.1.call-start
  7.2 0.7 all-gather.5.cloned.1.call-update
  7.9 0.7 fusion.32
  8.6 0.1 copy.49
  8.7 0.2 reduce_window_sum.11
  8.9 0.1 copy.50
  9.0 27.6 %all-gather.5.cloned.1.call-done = bf16[128,6144]{1,0:T(8,128)(2,1)} async-done(((bf16[128,768]{1,0:T(8,128)(2,1)}), bf16[128,6144]{1,0:T(8,128)(2,1)}) %all-gather.5.cloned.1.call-update) | async-done | bytes 1572880 | tf_op jit(solution)/shard_map/all_gather | solution.py:85
  36.5 2.6 convolution_convert_fusion.2
  39.1 5.8 broadcast_in_dim.8
  44.9 7.0 all-to-all-start.3
  51.9 0.0 all-gather.3.cloned.1.call-start
  51.9 0.7 all-gather.3.cloned.1.call-update
  52.6 26.5 %all-gather.3.cloned.1.call-done = bf16[128,6144]{1,0:T(8,128)(2,1)} async-done(((bf16[128,768]{1,0:T(8,128)(2,1)}), bf16[128,6144]{1,0:T(8,128)(2,1)}) %all-gather.3.cloned.1.call-update) | async-done | bytes 1572880 | tf_op jit(solution)/shard_map/all_gather | solution.py:86
  79.1 4.5 convolution_convert_fusion.3
  83.6 245.4 %all-to-all-done.3 = bf16[16,80,6144]{2,1,0:T(8,128)(2,1)} async-done(((bf16[16,80,6144]{2,1,0:T(8,128)(2,1)}), bf16[16,80,6144]{2,1,0:T(8,128)(2,1)}, u32[]{:S(2)}, u32[]{:S(2)}) %all-to-all-start.3) | async-done | bytes 15728672 | tf_op jit(solution)/shard_map/all_to_all | solution.py:89
  329.0 7.1 broadcast_in_dim.7
  336.0 0.0 copy-start
  336.0 10.0 %all-to-all-start.1 = ((bf16[16,80,6144]{2,1,0:T(8,128)(2,1)}), bf16[16,80,6144]{2,1,0:T(8,128)(2,1)}, u32[]{:S(2)}, u32[]{:S(2)}) async-start(bf16[16,80,6144]{2,1,0:T(8,128)(2,1)} %bitcast.48), calls=%async_computation.1 | async-start | bytes 31457280 | tf_op jit(solution)/shard_map/all_to_all | solution.py:92
  346.1 0.0 copy-done
  346.1 0.6 copy.52
  346.7 14.2 %fusion.33 = f32[1280,512]{0,1:T(8,128)} fusion(bf16[1280,6144]{1,0:T(8,128)(2,1)} %bitcast.15, bf16[6144,512]{1,0:T(8,128)(2,1)} %param.12), kind=kOutput, calls=%fused_computation.55 | convolution fusion | flops 8053063680 | bytes 24641536 | tf_op jit(solution)/shard_map/dot_general | solution.py:26
  360.9 261.8 %all-to-all-done.1 = bf16[16,80,6144]{2,1,0:T(8,128)(2,1)} async-done(((bf16[16,80,6144]{2,1,0:T(8,128)(2,1)}), bf16[16,80,6144]{2,1,0:T(8,128)(2,1)}, u32[]{:S(2)}, u32[]{:S(2)}) %all-to-all-start.1) | async-done | bytes 15728672 | tf_op jit(solution)/shard_map/all_to_all | solution.py:92
  622.7 0.0 copy-start.3
  622.7 0.0 copy-start.4
  622.7 16.9 %multiply_reduce_fusion = (bf16[1280]{0:T(1024)(128)(2,1)S(1)}, f32[1280,512]{0,1:T(8,128)}) fusion(f32[1280,512]{0,1:T(8,128)} %fusion.33, bf16[1280,512]{0,1:T(8,128)(2,1)S(1)} %copy.52, bf16[1280,6144]{1,0:T(8,128)(2,1)} %bitcast.9, bf16[512,6144]{1,0:T(8,128)(2,1)} %param.13), kind=kOutput, calls=%fused_computation.28 | convolution fusion | flops 8062237696 | bytes 28576256 | tf_op jit(solution)/shard_map/dot_general | solution.py:29
  639.6 0.1 convert_element_type.133
  639.7 19.2 %all_to_all.27 = bf16[16,1,80]{2,1,0:T(2,128)(2,1)S(1)} all-to-all(bf16[16,1,80]{2,1,0:T(2,128)(2,1)S(1)} %convert_element_type.133), channel_id=1, replica_groups=mesh['group'=16,'cuts'=8] {'group'}, dimensions={0} | all-to-all | bytes 5120 | tf_op jit(solution)/shard_map/all_to_all | solution.py:116
  658.9 0.2 fusion.17
  659.1 0.0 copy-done.3
  659.1 0.0 copy-done.4
  659.1 0.2 fusion.20
  659.4 10.6 %all_to_all.28 = bf16[16,1,80]{2,1,0:T(2,128)(2,1)S(1)} all-to-all(bf16[16,1,80]{2,1,0:T(2,128)(2,1)S(1)} %copy.51), channel_id=1, replica_groups=mesh['group'=16,'cuts'=8] {'group'}, dimensions={0} | all-to-all | bytes 5120 | tf_op jit(solution)/shard_map/all_to_all | solution.py:95
  670.0 0.1 reshape.81
  670.1 3.9 fusion.10
  674.0 0.0 copy-start.1
  674.0 15.0 %convolution_convert_fusion = bf16[1280,6144]{1,0:T(8,128)(2,1)} fusion(bf16[1280,512]{0,1:T(8,128)(2,1)S(1)} %get-tuple-element.38, bf16[6144,512]{1,0:T(8,128)(2,1)} %param.12), kind=kOutput, calls=%fused_computation.2 | convolution fusion | flops 8060928000 | bytes 23330816 | tf_op jit(solution)/shard_map/dot_general | solution.py:42
  689.0 0.0 copy-done.1
  689.0 5.1 all-to-all-start.2
  694.1 0.0 reduce-scatter.2.cloned.1.call-start
  694.2 14.0 %psum.7 = f32[128,2]{0,1:T(2,128)} all-reduce(f32[128,2]{0,1:T(2,128)S(1)} %get-tuple-element.35), channel_id=1, replica_groups=mesh['group'=16,'cuts'=8] {'cuts'}, use_global_device_ids=true, to_apply=%region_8.9 | all-reduce | flops 256 | bytes 2048 | tf_op jit(solution)/shard_map/psum | solution.py:129
  708.2 229.2 %all-to-all-done.2 = bf16[16,80,6144]{2,1,0:T(8,128)(2,1)} async-done(((bf16[16,80,6144]{2,1,0:T(8,128)(2,1)}), bf16[16,80,6144]{2,1,0:T(8,128)(2,1)}, u32[]{:S(2)}, u32[]{:S(2)}) %all-to-all-start.2) | async-done | bytes 15728672 | tf_op jit(solution)/shard_map/all_to_all | solution.py:109
  937.4 9.2 convert_reduce_fusion
  946.6 4.8 fusion.3
  951.3 0.0 reduce-scatter.2.cloned.1.call-update
  951.4 15.3 %fusion.2 = bf16[512,6144]{1,0:T(8,128)(2,1)} fusion(bf16[1280,6144]{1,0:T(8,128)(2,1)} %bitcast.9, f32[1280]{0:T(1024)S(1)} %reshape.81, f32[1280,512]{0,1:T(8,128)} %fusion.33, bf16[1280,512]{0,1:T(8,128)(2,1)S(1)} %copy.52), kind=kOutput, calls=%fused_computation.5 | convolution fusion | flops 8087011328 | bytes 25957376 | tf_op jit(solution)/shard_map/dot_general | solution.py:39
  966.7 0.0 copy-start.2
  966.7 1.5 copy.54
  968.2 0.0 copy-done.2
  968.2 16.5 %convolution_convert_fusion.1 = bf16[6144,512]{1,0:T(8,128)(2,1)} fusion(bf16[1280,6144]{1,0:T(8,128)(2,1)} %bitcast.15, bf16[1280,512]{0,1:T(8,128)(2,1)S(1)} %copy-done.2), kind=kOutput, calls=%fused_computation.6 | convolution fusion | flops 8056209408 | bytes 23330816 | tf_op jit(solution)/shard_map/dot_general | solution.py:36
  984.7 2.3 reduce-scatter.2.cloned.1.call-done
  (9 shorter events, 0.1 us)
Async XLA Ops:
  7.2 29.4 %all-gather.5.cloned.1.call-start = ((), (), s32[]{:S(2)}) async-start(), calls=%async_computation.8 | async-start | bytes 1769472 | tf_op jit(solution)/shard_map/all_gather | solution.py:85
  44.9 284.1 %all-to-all-start.3 = ((bf16[16,80,6144]{2,1,0:T(8,128)(2,1)}), bf16[16,80,6144]{2,1,0:T(8,128)(2,1)}, u32[]{:S(2)}, u32[]{:S(2)}) async-start(bf16[16,80,6144]{2,1,0:T(8,128)(2,1)} %bitcast.47), calls=%async_computation.4 | async-start | bytes 31457280 | tf_op jit(solution)/shard_map/all_to_all | solution.py:89
  51.9 27.2 %all-gather.3.cloned.1.call-start = ((), (), s32[]{:S(2)}) async-start(), calls=%async_computation.6 | async-start | bytes 1769472 | tf_op jit(solution)/shard_map/all_gather | solution.py:86
  336.0 10.0 %copy-start = (bf16[1280,512]{1,0:T(8,128)(2,1)S(1)}, bf16[1280,512]{1,0:T(8,128)(2,1)}, u32[]{:S(2)}) copy-start(bf16[1280,512]{1,0:T(8,128)(2,1)} %param.11) | copy-start | bytes 3932164
  336.0 286.7 %all-to-all-start.1 = ((bf16[16,80,6144]{2,1,0:T(8,128)(2,1)}), bf16[16,80,6144]{2,1,0:T(8,128)(2,1)}, u32[]{:S(2)}, u32[]{:S(2)}) async-start(bf16[16,80,6144]{2,1,0:T(8,128)(2,1)} %bitcast.48), calls=%async_computation.1 | async-start | bytes 31457280 | tf_op jit(solution)/shard_map/all_to_all | solution.py:92
  622.7 36.3 %copy-start.3 = (s32[128,2]{0,1:T(2,128)S(1)}, s32[128,2]{0,1:T(2,128)}, u32[]{:S(2)}) copy-start(s32[128,2]{0,1:T(2,128)} %param.9) | copy-start | bytes 3076
  622.7 36.4 %copy-start.4 = (f32[128,2]{0,1:T(2,128)S(1)}, f32[128,2]{0,1:T(2,128)}, u32[]{:S(2)}) copy-start(f32[128,2]{0,1:T(2,128)} %param.10) | copy-start | bytes 3076
  674.0 15.0 %copy-start.1 = (bf16[1280,512]{0,1:T(8,128)(2,1)}, bf16[1280,512]{0,1:T(8,128)(2,1)S(1)}, u32[]{:S(2)}) copy-start(bf16[1280,512]{0,1:T(8,128)(2,1)S(1)} %get-tuple-element.38) | copy-start | bytes 3932164
  689.0 248.4 %all-to-all-start.2 = ((bf16[16,80,6144]{2,1,0:T(8,128)(2,1)}), bf16[16,80,6144]{2,1,0:T(8,128)(2,1)}, u32[]{:S(2)}, u32[]{:S(2)}) async-start(bf16[16,80,6144]{2,1,0:T(8,128)(2,1)} %bitcast.49), calls=%async_computation.2 | async-start | bytes 31457280 | tf_op jit(solution)/shard_map/all_to_all | solution.py:109
  694.1 292.9 %reduce-scatter.2.cloned.1.call-start = ((), (), s32[]{:S(2)}) async-start(), calls=%async_computation.7 | async-start | bytes 1769472 | tf_op jit(solution)/shard_map/reduce_scatter | solution.py:125
  966.7 1.5 copy-start.2
Sparse Core Ops, SparseCore 0:
  9.7 26.7 all-gather.4
  54.4 24.6 all-gather.2
  951.5 35.4 reduce-scatter.1
where the time goes:
time: 994 us; the launch traced here: 993 us
  waiting for transfers between devices  794 us (80%)
  matrix products  90.2 us (9%)
  blocking collectives  43.8 us (4%)
  starting transfers between devices  22.2 us (2%)
  local copies, waits for them, and re-layouts  15.3 us (2%)
  other arithmetic  14.1 us (1%)
  between operations  13.9 us (1%)
    all_to_all x1, waiting for transfers between devices, body(): lax.all_to_all(place_rows(match, full_grad, copies), 'group', split_axis=...  262 us
    all_to_all x1, waiting for transfers between devices, body(): lax.all_to_all(place_rows(match, full_acts, copies), 'group', split_axis=...  245 us
    all_to_all x1, waiting for transfers between devices, body(): lax.all_to_all(slot_input.reshape(groups, MOST, width).astype(jnp.bfloat1...  229 us
    all_gather x1, waiting for transfers between devices, body(): lax.all_gather(acts, 'cuts', axis=1, tiled=True)  27.6 us
    all_gather x1, waiting for transfers between devices, body(): lax.all_gather(grad_out, 'cuts', axis=1, tiled=True)  26.5 us
  transfers between devices with their start and end apart: 6, of which 6 were waited for; matrix products, arithmetic and copies ran while one was open for 5% of the time, Pallas kernels for 0%

commit v1 on v0

v1 whole, which is shorter than its diff:
```python
import functools
import math

import jax
import jax.numpy as jnp
from jax import lax
from jax.experimental import pallas as pl
from jax.experimental.pallas import tpu as pltpu
from jax.sharding import Mesh
from jax.sharding import PartitionSpec as P

EXPERTS = 4
MOST = 80
SIDE = 4

bf16 = jnp.bfloat16
f32 = jnp.float32
hold = lax.optimization_barrier
root_coef = math.sqrt(2.0 / math.pi)


def gelu_pair(gate):
    inner = root_coef * (gate + 0.044715 * gate * gate * gate)
    tval = jnp.tanh(inner)
    act = 0.5 * gate * (1.0 + tval)
    slope = 0.5 * (1.0 + tval) + 0.5 * gate * (1.0 - tval * tval) * root_coef * (
        1.0 + 3.0 * 0.044715 * gate * gate
    )
    return (act, slope)


def go(v, axis, step):
    return lax.ppermute(v, axis, [(i, (i + step) % SIDE) for i in range(SIDE)])


def both(v, axis):
    return go(v, axis, 1), go(v, axis, -1)


def swap(v):
    return lax.ppermute(v, "c", [(0, 1), (1, 0)])


def add(*parts):
    total = parts[0].astype(f32)
    for part in parts[1:]:
        total = total + part.astype(f32)
    return total.astype(bf16)


def ring_far(left, right, axis):
    w = left.shape[1] // 2
    return go(left[:, :w], axis, 1), go(right[:, w:], axis, -1)


def join_rows(a, near, far):
    return jnp.concatenate([a, *near, jnp.concatenate(far, axis=1)], axis=0)


def join_cols(g, near, far):
    return jnp.concatenate([g, *near, *far], axis=1)


def cut(v, along):
    half = v.shape[along] // 2
    return (v[:half], v[half:]) if along == 0 else (v[:, :half], v[:, half:])


def widen(v, along, second):
    pads = [(0, 0), (0, 0)]
    pads[along] = (v.shape[along], 0) if second else (0, v.shape[along])
    return jnp.pad(v, pads)


def ring_all(own, left, right, opp, axis):
    return add(own, go(left, axis, -1), go(right, axis, 1), go(opp, axis, 2))


class PlaneSum:
    def __init__(self, mine, got):
        rows, cols = mine.shape
        self.n, k = rows // SIDE, cols // 2
        self.w = k // SIDE
        n, w = self.n, self.w

        def part(r0, r1, c0, c1):
            return mine[r0:r1, c0:c1], got[r0:r1, c0:c1]

        self.z = [part(i * n, (i + 1) * n, 0, k) for i in range(SIDE)]
        self.y = [part(0, rows, k + i * w, k + (i + 1) * w) for i in range(SIDE)]

    def first(self):
        za, zb = cut(add(*self.z[3]), 1)
        ya, yb = cut(add(*self.y[3]), 0)
        return go(za, "z", 1), go(zb, "z", -1), go(ya, "y", 1), go(yb, "y", -1)

    def second(self, met):
        za, zb, ya, yb = met
        return (
            go(add(*self.z[2], widen(za, 1, False)), "z", 1),
            go(add(*self.z[1], widen(zb, 1, True)), "z", -1),
            go(add(*self.y[2], widen(ya, 0, False)), "y", 1),
            go(add(*self.y[1], widen(yb, 0, True)), "y", -1),
        )

    def third(self, met):
        n, w = self.n, self.w
        one, two = add(*self.z[0], *met[:2]), add(*self.y[0], *met[2:])
        one = ring_all(*[one[:, i * w : (i + 1) * w] for i in range(SIDE)], "y")
        two = ring_all(*[two[i * n : (i + 1) * n] for i in range(SIDE)], "z")
        return jnp.concatenate([one, two], axis=1)


anyspec = pl.BlockSpec(memory_space=pl.ANY)
smem = pl.BlockSpec(memory_space=pltpu.SMEM)
dma = pltpu.SemaphoreType.DMA
sds = jax.ShapeDtypeStruct
NT = (((1,), (1,)), ((), ()))
TN = (((0,), (0,)), ((), ()))


def mul(a, b, dims):
    return lax.dot_general(a, b, dims, preferred_element_type=f32)


def params():
    return pltpu.CompilerParams(vmem_limit_bytes=56 * 2**20)


def cost(flops, moved):
    return pl.CostEstimate(flops=flops, bytes_accessed=moved, transcendentals=0)


def raw_kernel(tab, *refs):
    pieces, down = refs[:10], refs[10]
    raw_o, wg_o, g_v, w_v, raw_acc, s_g, s_w, s_o = refs[11:]
    copy = pltpu.make_async_copy
    n, half = pieces[0].shape
    blk = half // 4

    def grad_copies(ci):
        dst = [(0, 0, half), (1, 0, half), (2, 0, half), (3, 0, half // 2), (3, half // 2, half // 2)]
        return [
            copy(src, g_v.at[pl.ds(z * n, n), pl.ds(ci * half + c, m)], s_g.at[ci * 5 + i])
            for i, (src, (z, c, m)) in enumerate(zip(pieces[ci * 5 : ci * 5 + 5], dst))
        ]

    g_in = [grad_copies(0), grad_copies(1)]
    w_in = [
        copy(down.at[:, pl.ds(pl.multiple_of(tab[q] * blk, blk), blk)], w_v.at[q], s_w.at[q])
        for q in range(8)
    ]
    for ci in range(2):
        for cp in g_in[ci]:
            cp.start()
        for q in range(4):
            w_in[ci * 4 + q].start()
    last = [
        copy(g_v.at[:, pl.ds(ci * half, half)], wg_o.at[:, pl.ds(ci * half, half)], s_o.at[ci])
        for ci in range(2)
    ]
    for q in range(8):
        if q % 4 == 0:
            for cp in g_in[q // 4]:
                cp.wait()
            last[q // 4].start()
        w_in[q].wait()
        part = mul(g_v[:, q * blk : (q + 1) * blk], w_v[q], NT)
        if q == 0:
            raw_acc[...] = part
        else:
            raw_acc[...] += part
    last.append(copy(raw_acc, raw_o, s_o.at[2]))
    last[2].start()
    for cp in last:
        cp.wait()


def raw_call(tab, pieces, down):
    deep, wide = down.shape
    n = pieces[0].shape[0]
    rows = SIDE * n
    return pl.pallas_call(
        raw_kernel,
        out_shape=(sds((rows, deep), f32), sds((rows, wide), bf16)),
        in_specs=[smem] + [anyspec] * 11,
        out_specs=(anyspec,) * 2,
        scratch_shapes=[
            pltpu.VMEM((rows, wide), bf16),
            pltpu.VMEM((8, deep, wide // 8), bf16),
            pltpu.VMEM((rows, deep), f32),
            dma((10,)),
            dma((8,)),
            dma((3,)),
        ],
        compiler_params=params(),
        cost_estimate=cost(2 * rows * wide * deep, 2 * (2 * rows * wide + wide * deep)),
        name="raw_rows",
    )(tab, *pieces, down)


def main_kernel(*refs, first, whole):
    tab, acts, raw, gate, up = refs[:5]
    k = 5 if first else 6
    dup_o, hid_o, gg_o = refs[k : k + 3]
    outs = refs[k + 3 : k + 4] if whole else refs[k + 3 : k + 5]
    k += 4 if whole else 5
    a_v, v_v, gate_v, up_acc, raw_v, dup_v, hid_v, gg_v, o_v = refs[k : k + 9]
    s_a, s_v, s_gate, s_raw, s_gg, s_out, s_o = refs[k + 9 :]
    copy = pltpu.make_async_copy
    rows, blk = a_v.shape[1:]
    n, w = rows // SIDE, blk // 2

    a_in = [copy(acts.at[q], a_v.at[q], s_a.at[q]) for q in range(8)]
    v_in = [copy(up.at[pl.ds(q * blk, blk)], v_v.at[q], s_v.at[q]) for q in range(8)]
    raw_in = copy(raw, raw_v, s_raw.at[0])

    def gate_spot(i):
        return pl.ds(pl.multiple_of(tab[8 + i] * MOST, MOST), MOST)

    gate_in = [
        copy(gate.at[gate_spot(i)], gate_v.at[pl.ds(i * MOST, MOST)], s_gate.at[i])
        for i in range(8)
    ]
    gg_out = [
        copy(gg_v.at[pl.ds(i * MOST, MOST)], gg_o.at[gate_spot(i)], s_gg.at[i]) for i in range(8)
    ]
    for q in range(8):
        a_in[q].start()
        v_in[q].start()
    raw_in.start()
    for cp in gate_in:
        cp.start()
    for q in range(8):
        a_in[q].wait()
        v_in[q].wait()
        part = jnp.dot(a_v[q], v_v[q], preferred_element_type=f32)
        if q == 0:
            up_acc[...] = part
        else:
            up_acc[...] += part
    raw_in.wait()
    for cp in gate_in:
        cp.wait()

    def middle(i, carry):
        at = pl.ds(pl.multiple_of(i * MOST, MOST), MOST)
        act, slope = gelu_pair(gate_v[at, :].astype(f32))
        upv = up_acc[at, :]
        dhid = raw_v[at, :]
        hid_v[at, :] = (act * upv).astype(bf16)
        dup_v[at, :] = (dhid * act).astype(bf16)
        gg_v[at, :] = (dhid * upv * slope).astype(bf16)
        return carry

    lax.fori_loop(0, rows // MOST, middle, 0)
    side = gg_out + [copy(dup_v, dup_o, s_out.at[0]), copy(hid_v, hid_o, s_out.at[1])]
    for cp in side:
        cp.start()

    flying = [[], []]
    for turn, q in enumerate((4, 5, 6, 7, 0, 1, 2, 3)):
        slot = turn % 2
        for cp in flying[slot]:
            cp.wait()
        spot = tab[q]
        o_v[slot] = mul(dup_v[...], v_v[spot], NT).astype(bf16)
        if whole:
            flying[slot] = [
                copy(
                    o_v.at[slot, pl.ds(i * n, n)],
                    outs[0].at[pl.ds(pl.multiple_of((spot * SIDE + tab[16 + i]) * n, n), n)],
                    s_o.at[slot, i],
                )
                for i in range(SIDE)
            ]
        else:
            flying[slot] = [
                copy(
                    o_v.at[slot, :, pl.ds(h * w, w)],
                    outs[0 if q < 4 else 1].at[:, pl.ds(h * 4 * w + q % 4 * w, w)],
                    s_o.at[slot, h],
                )
                for h in range(2)
            ]
        for cp in flying[slot]:
            cp.start()
    for cp in flying[0] + flying[1] + side:
        cp.wait()


def main_call(tab, acts, raw, gate, up, gg, whole):
    wide, deep = up.shape
    rows, blk = acts.shape[1:]
    first = gg is None
    ins = [tab, acts, raw, gate, up] + ([] if first else [gg])
    sums = (
        (sds((rows * 8, blk), bf16),)
        if whole
        else (sds((rows, wide // 2), bf16), sds((rows, wide // 2), bf16))
    )
    return pl.pallas_call(
        functools.partial(main_kernel, first=first, whole=whole),
        out_shape=(sds((rows, deep), bf16), sds((rows, deep), bf16), sds(gate.shape, bf16)) + sums,
        in_specs=[smem] + [anyspec] * (len(ins) - 1),
        out_specs=(anyspec,) * (3 + len(sums)),
        scratch_shapes=[
            pltpu.VMEM((8, rows, blk), bf16),
            pltpu.VMEM((8, blk, deep), bf16),
            pltpu.VMEM((rows, deep), bf16),
            pltpu.VMEM((rows, deep), f32),
            pltpu.VMEM((rows, deep), f32),
            pltpu.VMEM((rows, deep), bf16),
            pltpu.VMEM((rows, deep), bf16),
            pltpu.VMEM((rows, deep), bf16),
            pltpu.VMEM((2, rows, blk), bf16),
            dma((8,)),
            dma((8,)),
            dma((8,)),
            dma((1,)),
            dma((8,)),
            dma((2,)),
            dma((2, 4)),
        ],
        input_output_aliases={} if first else {len(ins) - 1: 2},
        compiler_params=params(),
        cost_estimate=cost(4 * rows * wide * deep, 2 * (2 * rows * wide + wide * deep)),
        name="main_rows",
    )(*ins)


def up_grad_call(a0, a1, d0, d1, part, into):
    rows, blk = a0.shape[1:]
    deep = d0.shape[1]
    left = pl.BlockSpec((None, rows, blk), lambda q: (part * 4 + q, 0, 0))
    right = pl.BlockSpec((rows, deep), lambda q: (0, 0))

    def kernel(a0, a1, d0, d1, *rest):
        out = rest[-1]
        out[...] = (mul(a0[...], d0[...], TN) + mul(a1[...], d1[...], TN)).astype(bf16)

    more = () if into is None else (into,)
    return pl.pallas_call(
        kernel,
        out_shape=sds((8 * blk, deep), bf16),
        grid=(4,),
        in_specs=[left, left, right, right] + [anyspec] * len(more),
        out_specs=pl.BlockSpec((blk, deep), lambda q: (part * 4 + q, 0)),
        input_output_aliases={4: 0} if more else {},
        compiler_params=params(),
        cost_estimate=cost(rows * 8 * blk * deep * 2, 2 * rows * 8 * blk),
        name="up_grad",
    )(a0, a1, d0, d1, *more)


def down_grad_call(tab, g0, g1, h0, h1):
    rows, wide = g0.shape
    deep = h0.shape[1]
    blk = wide // 8
    right = pl.BlockSpec((rows, blk), lambda q, tab: (0, q))
    left = pl.BlockSpec((rows, deep), lambda q, tab: (0, 0))

    def kernel(tab, g0, g1, h0, h1, out):
        out[...] = (mul(h0[...], g0[...], TN) + mul(h1[...], g1[...], TN)).astype(bf16)

    return pl.pallas_call(
        kernel,
        out_shape=sds((deep, wide), bf16),
        grid_spec=pltpu.PrefetchScalarGridSpec(
            num_scalar_prefetch=1,
            grid=(8,),
            in_specs=[right, right, left, left],
            out_specs=pl.BlockSpec((deep, blk), lambda q, tab: (0, tab[q])),
        ),
        compiler_params=params(),
        cost_estimate=cost(rows * wide * deep * 4, 4 * rows * wide),
        name="down_grad",
    )(tab, g0, g1, h0, h1)


def body(acts, grad_out, expert_ids, combine, gate_pre, up_weight, down_weight):
    x, z, y, c = (lax.axis_index(name) for name in ("x", "z", "y", "c"))
    rel = jnp.arange(EXPERTS, dtype=jnp.int32)
    hit = expert_ids[:, :, None] == (x + rel) % EXPERTS
    member = jnp.any(hit, axis=1)
    wtab = jnp.sum(combine[:, :, None] * hit.astype(f32), axis=1)
    count = member.astype(jnp.int32)
    rank = jnp.cumsum(count, axis=0) - count
    places = jnp.arange(MOST, dtype=jnp.int32)
    found = member.T[:, None, :] & (rank.T[:, None, :] == places[None, :, None])
    match = found.astype(bf16).reshape(EXPERTS * MOST, -1)
    weight = jnp.sum(found.astype(f32) * wtab.T[:, None, :], axis=2).reshape(-1)
    used = jnp.any(found, axis=2).reshape(-1)

    slot_acts = jnp.dot(match, acts, preferred_element_type=f32).astype(bf16)
    slot_grad = jnp.dot(match, grad_out, preferred_element_type=f32)
    slot_wgrad = (weight[:, None] * slot_grad).astype(bf16)

    def send(k, step):
        rows = slice(k * MOST, (k + 1) * MOST)
        return go(jnp.concatenate([slot_acts[rows], slot_wgrad[rows]], axis=0), "x", step)

    back_1 = send(1, 1)
    back_3 = send(3, -1)
    back_2 = send(2, 2)
    a0 = jnp.concatenate([slot_acts[:MOST], back_1[:MOST]], axis=0)
    g0 = jnp.concatenate([slot_wgrad[:MOST], back_1[MOST:]], axis=0)
    a1 = jnp.concatenate([back_3[:MOST], back_2[:MOST]], axis=0)
    g1 = jnp.concatenate([back_3[MOST:], back_2[MOST:]], axis=0)

    ring = jnp.array([0, SIDE - 1, 1, 2], jnp.int32)
    ys, zs = (y + ring) % SIDE, (z + ring) % SIDE
    cols = jnp.concatenate([ys * 2 + c, ys * 2 + 1 - c])

    def table(d0, d1):
        xs = (x + jnp.array([d0, d1], jnp.int32)) % SIDE
        blocks = (xs[None, :] * SIDE + zs[:, None]).reshape(-1)
        return jnp.concatenate([cols, blocks, zs]).astype(jnp.int32)

    tab0, tab1 = table(0, 3), table(1, 2)

    a_near0, g_near0 = both(a0, "z"), both(g0, "y")
    a_near0, g_near0, a1, g1 = hold((a_near0, g_near0, a1, g1))
    a_far0, g_far0 = ring_far(*a_near0, "z"), ring_far(*g_near0, "y")
    a_far0, g_far0 = hold((a_far0, g_far0))
    s0, t0 = join_rows(a0, a_near0, a_far0), join_cols(g0, g_near0, g_far0)

    acts0 = lax.all_gather(s0, ("y", "c"), axis=0)
    near0, t0x = both(t0, "z"), swap(t0)
    g_near1 = both(g1, "y")
    g_near1, t0x, a1 = hold((g_near1, t0x, a1))
    g_far1 = ring_far(*g_near1, "y")
    g_far1, a1 = hold((g_far1, a1))
    t1 = join_cols(g1, g_near1, g_far1)
    a_near1 = both(a1, "z")
    near0, a_near1, t1 = hold((near0, a_near1, t1))
    far0, a_far1 = ring_far(*near0, "z"), ring_far(*a_near1, "z")
    far0, a_far1, t1 = hold((far0, a_far1, t1))
    s1 = join_rows(a1, a_near1, a_far1)
    acts1 = lax.all_gather(s1, ("y", "c"), axis=0)
    near1 = both(t1, "z")
    near0x, far0x = (swap(near0[0]), swap(near0[1])), (swap(far0[0]), swap(far0[1]))
    t1x = swap(t1)
    raw0, wg0 = raw_call(tab0, (t0, *near0, *far0, t0x, *near0x, *far0x), down_weight)
    near1, t1x, raw0 = hold((near1, t1x, raw0))
    far1, near1x = ring_far(*near1, "z"), (swap(near1[0]), swap(near1[1]))
    dup0, hid0, gg, sums0 = main_call(tab0, acts0, raw0, gate_pre, up_weight, None, True)
    far1, near1x, dup0, sums0 = hold((far1, near1x, dup0, sums0))
    sum0 = lax.psum_scatter(sums0, ("y", "c"), scatter_dimension=0, tiled=True)
    sum0 = lax.psum_scatter(sum0, "z", scatter_dimension=0, tiled=True)
    far1x = (swap(far1[0]), swap(far1[1]))
    raw1, wg1 = raw_call(tab1, (t1, *near1, *far1, t1x, *near1x, *far1x), down_weight)
    dup1, hid1, gg, mine1, other1 = main_call(tab1, acts1, raw1, gate_pre, up_weight, gg, False)
    got1 = swap(other1)
    grad_up = up_grad_call(acts0, acts1, dup0, dup1, 0, None)
    got1, grad_up = hold((got1, grad_up))
    sum1 = PlaneSum(mine1, got1)
    first1 = sum1.first()
    grad_up = up_grad_call(acts0, acts1, dup0, dup1, 1, grad_up)
    first1, grad_up = hold((first1, grad_up))
    second1 = sum1.second(first1)
    grad_down = down_grad_call(tab0, wg0, wg1, hid0, hid1)
    second1, grad_down = hold((second1, grad_down))
    sum1 = sum1.third(second1)
    sum1, sum0 = hold((sum1, sum0))

    home = jnp.concatenate(
        [
            sum0[:MOST],
            go(sum0[MOST:], "x", -1),
            go(sum1[MOST:], "x", 2),
            go(sum1[:MOST], "x", 1),
        ],
        axis=0,
    )
    own_input = mul(match, home, TN).astype(bf16)
    route = jnp.sum(home.astype(f32) * slot_acts.astype(f32), axis=1)
    route = jnp.where(used, route / jnp.where(used, weight, 1.0), 0.0).reshape(EXPERTS, MOST)
    token_route = jnp.sum(found.astype(f32) * route[:, :, None], axis=1).T
    terms = jnp.sum(token_route[:, None, :] * hit.astype(f32), axis=2)
    terms = terms + swap(terms)
    terms = (terms + go(terms, "y", 2)) + (go(terms, "y", 1) + go(terms, "y", -1))
    return (own_input, terms, grad_up, grad_down, gg)


def solution(mesh):
    grid = Mesh(mesh.devices.reshape(SIDE, SIDE, SIDE, 2), ("x", "z", "y", "c"))
    group, cuts, every = ("x", "z"), ("y", "c"), ("x", "z", "y", "c")
    return jax.shard_map(
        body,
        mesh=grid,
        in_specs=(
            P(group, cuts),
            P(group, cuts),
            P(group, None),
            P(group, None),
            P(None, every),
            P(None, every),
            P(every, None),
        ),
        out_specs=(
            P(group, cuts),
            P(group, None),
            P(None, every),
            P(every, None),
            P(None, every),
        ),
        check_vma=False,
    )
```

time: 994 us -> 294 us (0.30)
  waiting for transfers between devices: 794 us -> 80.7 us
  Pallas kernels: 0 us -> 90.2 us
  matrix products: 90.2 us -> 2.47 us
  starting transfers between devices: 22.2 us -> 73.6 us
  blocking collectives: 43.8 us -> 0 us
    all_to_all x3 -> x0, waiting for transfers between devices: 736 us -> none  [the longest x1 262 us: body(): lax.all_to_all(place_rows(match, full_grad, copies), 'group', split_axis=...]
    pallas_call x0 -> x7, Pallas kernels: none -> 90.2 us  [the longest x2 33.4 us: main_call(): pl.pallas_call(functools.partial(main_kernel, first=first, whole=whole),...]
    dot_general x10 -> x3, matrix products: 90.2 us -> 2.47 us  [the longest x1 1.21 us: body(): slot_grad = jnp.dot(match, grad_out, preferred_element_type=f32)]
    ppermute x0 -> x59, waiting for transfers between devices: none -> 80.5 us  [the longest x47 73.5 us: go(): return lax.ppermute(v, axis, [(i, (i + step) % SIDE) for i in range(SIDE)])]
    ppermute x0 -> x59, starting transfers between devices: none -> 73.5 us  [the longest x47 62.2 us: go(): return lax.ppermute(v, axis, [(i, (i + step) % SIDE) for i in range(SIDE)])]
    all_gather x2, waiting for transfers between devices: 54.1 us -> 0.02 us  [the longest x1 0.02 us: body(): acts1 = lax.all_gather(s1, ('y', 'c'), axis=0)]
    all_to_all x2 -> x0, blocking collectives: 29.7 us -> none  [the longest x1 19.2 us: body(): lax.all_to_all(slot_route.reshape(groups, MOST).astype(jnp.bfloat16), 'gr...]
    all_to_all x3 -> x0, starting transfers between devices: 22.1 us -> none  [the longest x1 10 us: body(): lax.all_to_all(place_rows(match, full_grad, copies), 'group', split_axis=...]
  transfers between devices with their start and end apart: 6 -> 63, of which waited for: 6 -> 33; matrix products, arithmetic and copies ran while one was open for 5% -> 7% of each run, Pallas kernels for 0% -> 31%
where the time goes in v1:
time: 294 us; the launch traced here: 288 us
  Pallas kernels  90.2 us (31%)
  waiting for transfers between devices  80.7 us (27%)
  starting transfers between devices  73.6 us (25%)
  other arithmetic  16.1 us (5%)
  between operations  14.6 us (5%)
  local copies, waits for them, and re-layouts  10.6 us (4%)
    ppermute x47, waiting for transfers between devices, go(): return lax.ppermute(v, axis, [(i, (i + step) % SIDE) for i in range(SIDE)])  73.5 us
    ppermute x47, starting transfers between devices, go(): return lax.ppermute(v, axis, [(i, (i + step) % SIDE) for i in range(SIDE)])  62.2 us
    pallas_call x2, Pallas kernels, main_call(): pl.pallas_call(functools.partial(main_kernel, first=first, whole=whole),...  33.4 us
    pallas_call x2, Pallas kernels, raw_call(): pl.pallas_call(raw_kernel, out_shape=(sds((rows, deep), f32), sds((rows,...  22.4 us
    pallas_call x2, Pallas kernels, up_grad_call(): pl.pallas_call(kernel, out_shape=sds((8 * blk, deep), bf16), grid=(4,), i...  18 us
    pallas_call x1, Pallas kernels, down_grad_call(): pl.pallas_call(kernel, out_shape=sds((deep, wide), bf16), grid_spec=pltpu...  16.3 us
    ppermute x12, starting transfers between devices, swap(): return lax.ppermute(v, 'c', [(0, 1), (1, 0)])  11.3 us
    convert_element_type x8, other arithmetic, add(): return total.astype(bf16)  10.3 us
  transfers between devices with their start and end apart: 63, of which 33 were waited for; matrix products, arithmetic and copies ran while one was open for 7% of the time, Pallas kernels for 31%

profile of v1, /device:TPU:0, one launch (start us, length us, event | category | flops | bytes accessed | tf_op | source)
XLA Modules:
  0.0 288.2 jit_solution(17483682610734446)
XLA Ops:
  9.9 1.2 fusion
  11.3 1.6 collective-permute-start
  12.9 1.7 collective-permute-start.5
  14.7 2.0 collective-permute-start.6
  16.7 3.5 %collective-permute-done = bf16[160,768]{1,0:T(8,128)(2,1)S(1)} collective-permute-done((bf16[160,768]{1,0:T(8,128)(2,1)S(1)}, bf16[160,768]{1,0:T(8,128)(2,1)S(1)}, u32[]{:S(2)}, u32[]{:S(2)}) %collective-permute-start) | collective-permute-done | bytes 245792 | tf_op jit(solution)/shard_map/ppermute | solution.py:33
  20.2 4.5 %collective-permute-start.2 = (bf16[160,768]{1,0:T(8,128)(2,1)S(1)}, bf16[160,768]{1,0:T(8,128)(2,1)S(1)}, u32[]{:S(2)}, u32[]{:S(2)}) collective-permute-start(bf16[160,768]{1,0:T(8,128)(2,1)S(1)} %pad_maximum_fusion.2), channel_id=1, source_target_pairs={{0,24},{8,0},{16,8},{24,16},{1,25},{9,1},{17,9},{25,17},{2,26},{10... | collective-permute-start | bytes 737288 | tf_op jit(solution)/shard_map/ppermute | solution.py:33
  25.4 3.0 %collective-permute-start.4 = (bf16[160,768]{1,0:T(8,128)(2,1)S(1)}, bf16[160,768]{1,0:T(8,128)(2,1)S(1)}, u32[]{:S(2)}, u32[]{:S(2)}) collective-permute-start(bf16[160,768]{1,0:T(8,128)(2,1)S(1)} %get-tuple-element.169), channel_id=1, source_target_pairs={{0,6},{2,0},{4,2},{6,4},{1,7},{3,1},{5,3},{7,5},{8,14},{10,8},{12,... | collective-permute-start | bytes 737288 | tf_op jit(solution)/shard_map/ppermute | solution.py:33
  28.8 3.4 %collective-permute-done.1 = bf16[160,768]{1,0:T(8,128)(2,1)S(1)} collective-permute-done((bf16[160,768]{1,0:T(8,128)(2,1)S(1)}, bf16[160,768]{1,0:T(8,128)(2,1)S(1)}, u32[]{:S(2)}, u32[]{:S(2)}) %collective-permute-start.1) | collective-permute-done | bytes 245792 | tf_op jit(solution)/shard_map/ppermute | solution.py:33
  32.3 3.5 %collective-permute-done.3 = bf16[160,768]{1,0:T(8,128)(2,1)S(1)} collective-permute-done((bf16[160,768]{1,0:T(8,128)(2,1)S(1)}, bf16[160,768]{1,0:T(8,128)(2,1)S(1)}, u32[]{:S(2)}, u32[]{:S(2)}) %collective-permute-start.3) | collective-permute-done | bytes 245792 | tf_op jit(solution)/shard_map/ppermute | solution.py:33
  35.9 3.3 %collective-permute-start.10 = (bf16[160,384]{1,0:T(8,128)(2,1)S(1)}, bf16[160,384]{1,0:T(8,128)(2,1)S(1)}, u32[]{:S(2)}, u32[]{:S(2)}) collective-permute-start(bf16[160,384]{1,0:T(8,128)(2,1)S(1)} %slice.189), channel_id=1, source_target_pairs={{0,24},{8,0},{16,8},{24,16},{1,25},{9,1},{17,9},{25,17},{2,26},{10... | collective-permute-start | bytes 368648 | tf_op jit(solution)/shard_map/ppermute | solution.py:33
  39.2 2.0 collective-permute-start.11
  41.6 3.6 %collective-permute-done.9 = bf16[160,384]{1,0:T(8,128)(2,1)S(1)} collective-permute-done((bf16[160,384]{1,0:T(8,128)(2,1)S(1)}, bf16[160,384]{1,0:T(8,128)(2,1)S(1)}, u32[]{:S(2)}, u32[]{:S(2)}) %collective-permute-start.9) | collective-permute-done | bytes 122912 | tf_op jit(solution)/shard_map/ppermute | solution.py:33
  49.1 3.2 %collective-permute-start.17 = (bf16[160,3072]{1,0:T(8,128)(2,1)}, bf16[160,3072]{1,0:T(8,128)(2,1)S(1)}, u32[]{:S(2)}, u32[]{:S(2)}) collective-permute-start(bf16[160,3072]{1,0:T(8,128)(2,1)} %constant_dynamic-update-slice_fusion.refs_0_), channel_id=1, source_target_pairs={{0,24},{8,0},{16,8},{24,16},{1,25},{9,1},{17,9},{25,17},{2,26},{10... | collective-permute-start | bytes 2949128 | tf_op jit(solution)/shard_map/ppermute | solution.py:33
  52.3 2.0 collective-permute-start.7
  54.4 8.1 %collective-permute-done.8 = bf16[160,768]{1,0:T(8,128)(2,1)S(1)} collective-permute-done((bf16[160,768]{1,0:T(8,128)(2,1)S(1)}, bf16[160,768]{1,0:T(8,128)(2,1)S(1)}, u32[]{:S(2)}, u32[]{:S(2)}) %collective-permute-start.8) | collective-permute-done | bytes 245792 | tf_op jit(solution)/shard_map/ppermute | solution.py:33
  62.5 1.8 collective-permute-done.7
  64.4 2.6 collective-permute-start.14
  67.0 5.5 %collective-permute-done.15 = bf16[160,384]{1,0:T(8,128)(2,1)S(1)} collective-permute-done((bf16[160,384]{1,0:T(8,128)(2,1)S(1)}, bf16[160,384]{1,0:T(8,128)(2,1)S(1)}, u32[]{:S(2)}, u32[]{:S(2)}) %collective-permute-start.15) | collective-permute-done | bytes 122912 | tf_op jit(solution)/shard_map/ppermute | solution.py:33
  73.5 2.9 %collective-permute-start.19 = (bf16[160,768]{1,0:T(8,128)(2,1)S(1)}, bf16[160,768]{1,0:T(8,128)(2,1)S(1)}, u32[]{:S(2)}, u32[]{:S(2)}) collective-permute-start(bf16[160,768]{1,0:T(8,128)(2,1)S(1)} %pad_maximum_fusion.6), channel_id=1, source_target_pairs={{0,24},{8,0},{16,8},{24,16},{1,25},{9,1},{17,9},{25,17},{2,26},{10... | collective-permute-start | bytes 737288 | tf_op jit(solution)/shard_map/ppermute | solution.py:33
  76.6 1.8 collective-permute-done.16.refs_1_
  78.3 1.8 collective-permute-done.19
  80.2 3.7 %collective-permute-done.18 = bf16[160,768]{1,0:T(8,128)(2,1)S(1)} collective-permute-done((bf16[160,768]{1,0:T(8,128)(2,1)S(1)}, bf16[160,768]{1,0:T(8,128)(2,1)S(1)}, u32[]{:S(2)}, u32[]{:S(2)}) %collective-permute-start.18) | collective-permute-done | bytes 245792 | tf_op jit(solution)/shard_map/ppermute | solution.py:33
  84.0 2.0 collective-permute-start.20
  86.1 1.4 collective-permute-start.23
  88.2 8.2 %collective-permute-done.23 = bf16[160,384]{1,0:T(8,128)(2,1)S(1)} collective-permute-done((bf16[160,384]{1,0:T(8,128)(2,1)S(1)}, bf16[160,384]{1,0:T(8,128)(2,1)S(1)}, u32[]{:S(2)}, u32[]{:S(2)}) %collective-permute-start.23) | collective-permute-done | bytes 122912 | tf_op jit(solution)/shard_map/ppermute | solution.py:33
  96.4 1.3 collective-permute-done.22
  101.9 1.3 collective-permute-done.30.refs_9_
  104.6 1.9 collective-permute-done.28.refs_7_
  106.6 11.5 %raw_rows.2 = (f32[640,512]{1,0:T(8,128)}, bf16[640,6144]{1,0:T(8,128)(2,1)}) custom-call(s32[20]{0:T(128)} %get-tuple-element.171.tab.refs_0_, bf16[160,3072]{1,0:T(8,128)(2,1)} %constant_dynamic-update-slice_fusion.refs_0_, bf16[160,3072]{1,0:T(8,128)(2,1)} %copy-done.5, bf16[160,3072]{1,0:T(8,128)(2,1)} %copy-done.4, ...), custom_call_target="tpu_custom_call" | custom-call | flops 4026531840 | bytes 22020096 | tf_op jit(solution)/shard_map/raw_rows/pallas_call | solution.py:183
  118.1 7.7 %collective-permute-done.25.refs_2_ = bf16[160,3072]{1,0:T(8,128)(2,1)} collective-permute-done((bf16[160,3072]{1,0:T(8,128)(2,1)}, bf16[160,3072]{1,0:T(8,128)(2,1)}, u32[]{:S(2)}, u32[]{:S(2)}) %collective-permute-start.25) | collective-permute-done | bytes 983072 | tf_op jit(solution)/shard_map/ppermute | solution.py:33
  125.8 2.7 collective-permute-done.24.refs_1_
  130.1 1.1 slice.199
  131.3 2.0 collective-permute-start.31
  133.3 16.6 %main_rows.2 = (bf16[640,512]{1,0:T(8,128)(2,1)}, bf16[640,512]{1,0:T(8,128)(2,1)}, bf16[1280,512]{1,0:T(8,128)(2,1)}, bf16[5120,768]{1,0:T(8,128)(2,1)}) custom-call(s32[20]{0:T(128)} %get-tuple-element.171.tab.refs_0_, bf16[8,640,768]{2,1,0:T(8,128)(2,1)} %bitcast.19, f32[640,512]{1,0:T(8,128)} %get-tuple-element.99.refs_2_, bf16[1280,512]{1,0:T(8,128)(2,1)} %refs_3_.3, ...), custom_call_target="tpu_custom_call" | custom-call | flops 8053063680 | bytes 22020096 | tf_op jit(solution)/shard_map/main_rows/pallas_call | solution.py:302
  151.0 8.6 %collective-permute-start.35 = (bf16[160,1536]{1,0:T(8,128)(2,1)}, bf16[160,1536]{1,0:T(8,128)(2,1)S(1)}, u32[]{:S(2)}, u32[]{:S(2)}) collective-permute-start(bf16[160,1536]{1,0:T(8,128)(2,1)} %collective-permute-done.31.refs_3_), channel_id=1, source_target_pairs={{0,1},{1,0},{2,3},{3,2},{4,5},{5,4},{6,7},{7,6},{8,9},{9,8},{10,11... | collective-permute-start | bytes 1474568 | tf_op jit(solution)/shard_map/ppermute | solution.py:41
  160.1 1.6 collective-permute-done.35.refs_8_
  162.9 10.9 %raw_rows.3 = (f32[640,512]{1,0:T(8,128)}, bf16[640,6144]{1,0:T(8,128)(2,1)}) custom-call(s32[20]{0:T(128)} %get-tuple-element.172.tab.refs_0_, bf16[160,3072]{1,0:T(8,128)(2,1)} %copy-done.6, bf16[160,3072]{1,0:T(8,128)(2,1)} %collective-permute-done.24.refs_1_, bf16[160,3072]{1,0:T(8,128)(2,1)} %collective-permute-done.25.refs_2_, ...), custom_call_target="tpu_custom_call" | custom-call | flops 4026531840 | bytes 22020096 | tf_op jit(solution)/shard_map/raw_rows/pallas_call | solution.py:183
  173.8 16.8 %main_rows.3 = (bf16[640,512]{1,0:T(8,128)(2,1)}, bf16[640,512]{1,0:T(8,128)(2,1)}, bf16[1280,512]{1,0:T(8,128)(2,1)}, bf16[640,3072]{1,0:T(8,128)(2,1)}, bf16[640,3072]{1,0:T(8,128)(2,1)}) custom-call(s32[20]{0:T(128)} %get-tuple-element.172.tab.refs_0_, bf16[8,640,768]{2,1,0:T(8,128)(2,1)} %bitcast.22, ...), custom_call_target="tpu_custom_call", output_to_operand_aliasing={{2}: (5, {})} | custom-call | flops 8053063680 | bytes 22020096 | tf_op jit(solution)/shard_map/main_rows/pallas_call | solution.py:302
  190.9 9.1 %up_grad.2.rest_0_ = bf16[6144,512]{1,0:T(8,128)(2,1)} custom-call(bf16[8,640,768]{2,1,0:T(8,128)(2,1)} %bitcast.20, bf16[8,640,768]{2,1,0:T(8,128)(2,1)} %bitcast.23, bf16[640,512]{1,0:T(8,128)(2,1)} %get-tuple-element.111.d0, bf16[640,512]{1,0:T(8,128)(2,1)} %get-tuple-element.112.d1), custom_call_target="tpu_custom_call" | custom-call | flops 4026531840 | bytes 7864320 | tf_op jit(solution)/shard_map/up_grad/pallas_call | solution.py:343
  200.0 1.2 add_convert_fusion.6
  201.2 2.1 collective-permute-start.41
  203.4 1.2 add_convert_fusion.7
  204.6 2.6 collective-permute-start.39
  207.1 8.9 %up_grad.3 = bf16[6144,512]{1,0:T(8,128)(2,1)} custom-call(bf16[8,640,768]{2,1,0:T(8,128)(2,1)} %bitcast.21, bf16[8,640,768]{2,1,0:T(8,128)(2,1)} %bitcast.24, bf16[640,512]{1,0:T(8,128)(2,1)} %get-tuple-element.111.d0, bf16[640,512]{1,0:T(8,128)(2,1)} %get-tuple-element.112.d1, bf16[6144,512]{1,0:T(8,128)(2,1)} %up_grad.2.rest_0_), custom_call_target="tpu_custom_call", output_to_operand_aliasing={{}: (4, {})} | custom-call | flops 4026531840 | bytes 7864320 | tf_op jit(solution)/shard_map/up_grad/pallas_call | solution.py:343
  216.1 2.3 add_convert_fusion.4
  218.4 3.2 %collective-permute-start.43 = (bf16[160,1536]{1,0:T(8,128)(2,1)}, bf16[160,1536]{1,0:T(8,128)(2,1)S(1)}, u32[]{:S(2)}, u32[]{:S(2)}) collective-permute-start(bf16[160,1536]{1,0:T(8,128)(2,1)} %get-tuple-element.137), channel_id=1, source_target_pairs={{0,24},{8,0},{16,8},{24,16},{1,25},{9,1},{17,9},{25,17},{2,26},{10... | collective-permute-start | bytes 1474568 | tf_op jit(solution)/shard_map/ppermute | solution.py:33
  221.6 2.5 add_convert_fusion.2
  224.1 1.8 collective-permute-start.45
  226.2 16.3 %down_grad.1 = bf16[512,6144]{1,0:T(8,128)(2,1)} custom-call(s32[20]{0:T(128)} %get-tuple-element.171.tab.refs_0_, bf16[640,6144]{1,0:T(8,128)(2,1)} %get-tuple-element.119.g0, bf16[640,6144]{1,0:T(8,128)(2,1)} %get-tuple-element.120.g1, bf16[640,512]{1,0:T(8,128)(2,1)} %get-tuple-element.121.h0, bf16[640,512]{1,0:T(8,128)(2,1)} %get-tuple-element.122.h1), custom_call_target="tpu_custom_call" | custom-call | flops 8053063680 | bytes 15728640 | tf_op jit(solution)/shard_map/down_grad/pallas_call | solution.py:366
  242.6 1.5 add_convert_fusion
  244.1 3.3 %collective-permute-start.49 = (bf16[160,384]{1,0:T(8,128)(2,1)S(1)}, bf16[160,384]{1,0:T(8,128)(2,1)S(1)}, u32[]{:S(2)}, u32[]{:S(2)}) collective-permute-start(bf16[160,384]{1,0:T(8,128)(2,1)S(1)} %get-tuple-element.142), channel_id=1, source_target_pairs={{0,24},{8,0},{16,8},{24,16},{1,25},{9,1},{17,9},{25,17},{2,26},{10... | collective-permute-start | bytes 368648 | tf_op jit(solution)/shard_map/ppermute | solution.py:33
  248.4 1.5 add_convert_fusion.1
  249.9 2.8 collective-permute-start.46
  253.0 1.3 collective-permute-start.47
  255.1 4.0 %collective-permute-done.48 = bf16[160,384]{1,0:T(8,128)(2,1)S(1)} collective-permute-done((bf16[160,384]{1,0:T(8,128)(2,1)S(1)}, bf16[160,384]{1,0:T(8,128)(2,1)S(1)}, u32[]{:S(2)}, u32[]{:S(2)}) %collective-permute-start.48) | collective-permute-done | bytes 122912 | tf_op jit(solution)/shard_map/ppermute | solution.py:33
  259.2 1.2 collective-permute-done.47
  261.5 2.8 collective-permute-start.52
  264.7 1.3 collective-permute-start.54
  266.8 4.1 %collective-permute-done.53 = bf16[80,768]{1,0:T(8,128)(2,1)S(1)} collective-permute-done((bf16[80,768]{1,0:T(8,128)(2,1)S(1)}, bf16[80,768]{1,0:T(8,128)(2,1)S(1)}, u32[]{:S(2)}, u32[]{:S(2)}) %collective-permute-start.53) | collective-permute-done | bytes 122912 | tf_op jit(solution)/shard_map/ppermute | solution.py:33
  270.9 1.2 collective-permute-done.54
  272.7 1.1 collective-permute-done.55
  274.7 1.1 collective-permute-start.57
  277.8 1.6 collective-permute-done.57
  279.5 1.4 collective-permute-done.56
  (187 shorter events, 29.5 us)
Async XLA Ops:
  7.2 126.1 %all-gather.7.cloned.1.call-start = ((), (), s32[]{:S(2)}) async-start(), calls=%async_computation.5 | async-start | bytes 8847360 | tf_op jit(solution)/shard_map/all_gather | solution.py:428
  11.3 8.9 %collective-permute-start = (bf16[160,768]{1,0:T(8,128)(2,1)S(1)}, bf16[160,768]{1,0:T(8,128)(2,1)S(1)}, u32[]{:S(2)}, u32[]{:S(2)}) collective-permute-start(bf16[160,768]{1,0:T(8,128)(2,1)S(1)} %pad_maximum_fusion.1), channel_id=1, source_target_pairs={{0,32},{32,64},{64,96},{96,0},{1,33},{33,65},{65,97},{97,1},{2,34}... | collective-permute-start | bytes 737288 | tf_op jit(solution)/shard_map/ppermute | solution.py:33
  12.9 15.5 %collective-permute-start.5 = (bf16[160,768]{1,0:T(8,128)(2,1)S(1)}, bf16[160,768]{1,0:T(8,128)(2,1)S(1)}, u32[]{:S(2)}, u32[]{:S(2)}) collective-permute-start(bf16[160,768]{1,0:T(8,128)(2,1)S(1)} %pad_maximum_fusion.4), channel_id=1, source_target_pairs={{0,96},{32,0},{64,32},{96,64},{1,97},{33,1},{65,33},{97,65},{2,98}... | collective-permute-start | bytes 737288 | tf_op jit(solution)/shard_map/ppermute | solution.py:33
  14.7 13.7 %collective-permute-start.6 = (bf16[160,768]{1,0:T(8,128)(2,1)S(1)}, bf16[160,768]{1,0:T(8,128)(2,1)S(1)}, u32[]{:S(2)}, u32[]{:S(2)}) collective-permute-start(bf16[160,768]{1,0:T(8,128)(2,1)S(1)} %pad_maximum_fusion.5), channel_id=1, source_target_pairs={{0,64},{32,96},{64,0},{96,32},{1,65},{33,97},{65,1},{97,33},{2,66}... | collective-permute-start | bytes 737288 | tf_op jit(solution)/shard_map/ppermute | solution.py:33
  20.2 8.6 %collective-permute-start.2 = (bf16[160,768]{1,0:T(8,128)(2,1)S(1)}, bf16[160,768]{1,0:T(8,128)(2,1)S(1)}, u32[]{:S(2)}, u32[]{:S(2)}) collective-permute-start(bf16[160,768]{1,0:T(8,128)(2,1)S(1)} %pad_maximum_fusion.2), channel_id=1, source_target_pairs={{0,24},{8,0},{16,8},{24,16},{1,25},{9,1},{17,9},{25,17},{2,26},{10... | collective-permute-start | bytes 737288 | tf_op jit(solution)/shard_map/ppermute | solution.py:33
  24.6 7.6 %collective-permute-start.1 = (bf16[160,768]{1,0:T(8,128)(2,1)S(1)}, bf16[160,768]{1,0:T(8,128)(2,1)S(1)}, u32[]{:S(2)}, u32[]{:S(2)}) collective-permute-start(bf16[160,768]{1,0:T(8,128)(2,1)S(1)} %pad_maximum_fusion.2), channel_id=1, source_target_pairs={{0,8},{8,16},{16,24},{24,0},{1,9},{9,17},{17,25},{25,1},{2,10},{10... | collective-permute-start | bytes 737288 | tf_op jit(solution)/shard_map/ppermute | solution.py:33
  25.4 6.9 %collective-permute-start.4 = (bf16[160,768]{1,0:T(8,128)(2,1)S(1)}, bf16[160,768]{1,0:T(8,128)(2,1)S(1)}, u32[]{:S(2)}, u32[]{:S(2)}) collective-permute-start(bf16[160,768]{1,0:T(8,128)(2,1)S(1)} %get-tuple-element.169), channel_id=1, source_target_pairs={{0,6},{2,0},{4,2},{6,4},{1,7},{3,1},{5,3},{7,5},{8,14},{10,8},{12,... | collective-permute-start | bytes 737288 | tf_op jit(solution)/shard_map/ppermute | solution.py:33
  28.4 7.4 %collective-permute-start.3 = (bf16[160,768]{1,0:T(8,128)(2,1)S(1)}, bf16[160,768]{1,0:T(8,128)(2,1)S(1)}, u32[]{:S(2)}, u32[]{:S(2)}) collective-permute-start(bf16[160,768]{1,0:T(8,128)(2,1)S(1)} %get-tuple-element.169), channel_id=1, source_target_pairs={{0,2},{2,4},{4,6},{6,0},{1,3},{3,5},{5,7},{7,1},{8,10},{10,12},{12... | collective-permute-start | bytes 737288 | tf_op jit(solution)/shard_map/ppermute | solution.py:33
  35.9 5.7 %collective-permute-start.10 = (bf16[160,384]{1,0:T(8,128)(2,1)S(1)}, bf16[160,384]{1,0:T(8,128)(2,1)S(1)}, u32[]{:S(2)}, u32[]{:S(2)}) collective-permute-start(bf16[160,384]{1,0:T(8,128)(2,1)S(1)} %slice.189), channel_id=1, source_target_pairs={{0,24},{8,0},{16,8},{24,16},{1,25},{9,1},{17,9},{25,17},{2,26},{10... | collective-permute-start | bytes 368648 | tf_op jit(solution)/shard_map/ppermute | solution.py:33
  39.2 6.1 %collective-permute-start.9 = (bf16[160,384]{1,0:T(8,128)(2,1)S(1)}, bf16[160,384]{1,0:T(8,128)(2,1)S(1)}, u32[]{:S(2)}, u32[]{:S(2)}) collective-permute-start(bf16[160,384]{1,0:T(8,128)(2,1)S(1)} %slice.188), channel_id=1, source_target_pairs={{0,8},{8,16},{16,24},{24,0},{1,9},{9,17},{17,25},{25,1},{2,10},{10... | collective-permute-start | bytes 368648 | tf_op jit(solution)/shard_map/ppermute | solution.py:33
  39.2 6.1 %collective-permute-start.12 = (bf16[160,384]{1,0:T(8,128)(2,1)S(1)}, bf16[160,384]{1,0:T(8,128)(2,1)S(1)}, u32[]{:S(2)}, u32[]{:S(2)}) collective-permute-start(bf16[160,384]{1,0:T(8,128)(2,1)S(1)} %slice.191), channel_id=1, source_target_pairs={{0,6},{2,0},{4,2},{6,4},{1,7},{3,1},{5,3},{7,5},{8,14},{10,8},{12,... | collective-permute-start | bytes 368648 | tf_op jit(solution)/shard_map/ppermute | solution.py:33
  39.2 6.1 %collective-permute-start.11 = (bf16[160,384]{1,0:T(8,128)(2,1)S(1)}, bf16[160,384]{1,0:T(8,128)(2,1)S(1)}, u32[]{:S(2)}, u32[]{:S(2)}) collective-permute-start(bf16[160,384]{1,0:T(8,128)(2,1)S(1)} %slice.190), channel_id=1, source_target_pairs={{0,2},{2,4},{4,6},{6,0},{1,3},{3,5},{5,7},{7,1},{8,10},{10,12},{12... | collective-permute-start | bytes 368648 | tf_op jit(solution)/shard_map/ppermute | solution.py:33
  46.3 127.5 %all-gather.5.cloned.1.call-start = ((), (), s32[]{:S(2)}) async-start(), calls=%async_computation.4 | async-start | bytes 8847360 | tf_op jit(solution)/shard_map/all_gather | solution.py:440
  49.1 54.7 %copy-start.9 = (s32[2]{0:T(128)S(1)}, s32[2]{0:T(128)}, u32[]{:S(2)}) copy-start(s32[2]{0:T(128)} %constant.83.clone) | copy-start | bytes 28
  49.1 15.2 %collective-permute-start.13 = (bf16[160,3072]{1,0:T(8,128)(2,1)}, bf16[160,3072]{1,0:T(8,128)(2,1)}, u32[]{:S(2)}, u32[]{:S(2)}) collective-permute-start(bf16[160,3072]{1,0:T(8,128)(2,1)} %constant_dynamic-update-slice_fusion.refs_0_), channel_id=1, source_target_pairs={{0,1},{1,0},{2,3},{3,2},{4,5},{5,4},{6,7},{7,6},{8,9},{9,8},{10,11... | collective-permute-start | bytes 2949128 | tf_op jit(solution)/shard_map/ppermute | solution.py:41
  49.1 27.5 %collective-permute-start.17 = (bf16[160,3072]{1,0:T(8,128)(2,1)}, bf16[160,3072]{1,0:T(8,128)(2,1)S(1)}, u32[]{:S(2)}, u32[]{:S(2)}) collective-permute-start(bf16[160,3072]{1,0:T(8,128)(2,1)} %constant_dynamic-update-slice_fusion.refs_0_), channel_id=1, source_target_pairs={{0,24},{8,0},{16,8},{24,16},{1,25},{9,1},{17,9},{25,17},{2,26},{10... | collective-permute-start | bytes 2949128 | tf_op jit(solution)/shard_map/ppermute | solution.py:33
  52.3 26.0 %collective-permute-start.16 = (bf16[160,3072]{1,0:T(8,128)(2,1)}, bf16[160,3072]{1,0:T(8,128)(2,1)S(1)}, u32[]{:S(2)}, u32[]{:S(2)}) collective-permute-start(bf16[160,3072]{1,0:T(8,128)(2,1)} %constant_dynamic-update-slice_fusion.refs_0_), channel_id=1, source_target_pairs={{0,8},{8,16},{16,24},{24,0},{1,9},{9,17},{17,25},{25,1},{2,10},{10... | collective-permute-start | bytes 2949128 | tf_op jit(solution)/shard_map/ppermute | solution.py:33
  52.3 10.2 %collective-permute-start.8 = (bf16[160,768]{1,0:T(8,128)(2,1)S(1)}, bf16[160,768]{1,0:T(8,128)(2,1)S(1)}, u32[]{:S(2)}, u32[]{:S(2)}) collective-permute-start(bf16[160,768]{1,0:T(8,128)(2,1)S(1)} %pad_maximum_fusion.7), channel_id=1, source_target_pairs={{0,6},{2,0},{4,2},{6,4},{1,7},{3,1},{5,3},{7,5},{8,14},{10,8},{12,... | collective-permute-start | bytes 737288 | tf_op jit(solution)/shard_map/ppermute | solution.py:33
  52.3 11.9 %collective-permute-start.7 = (bf16[160,768]{1,0:T(8,128)(2,1)S(1)}, bf16[160,768]{1,0:T(8,128)(2,1)S(1)}, u32[]{:S(2)}, u32[]{:S(2)}) collective-permute-start(bf16[160,768]{1,0:T(8,128)(2,1)S(1)} %pad_maximum_fusion.7), channel_id=1, source_target_pairs={{0,2},{2,4},{4,6},{6,0},{1,3},{3,5},{5,7},{7,1},{8,10},{10,12},{12... | collective-permute-start | bytes 737288 | tf_op jit(solution)/shard_map/ppermute | solution.py:33
  64.3 8.2 %collective-permute-start.15 = (bf16[160,384]{1,0:T(8,128)(2,1)S(1)}, bf16[160,384]{1,0:T(8,128)(2,1)S(1)}, u32[]{:S(2)}, u32[]{:S(2)}) collective-permute-start(bf16[160,384]{1,0:T(8,128)(2,1)S(1)} %slice.193), channel_id=1, source_target_pairs={{0,6},{2,0},{4,2},{6,4},{1,7},{3,1},{5,3},{7,5},{8,14},{10,8},{12,... | collective-permute-start | bytes 368648 | tf_op jit(solution)/shard_map/ppermute | solution.py:33
  64.4 9.1 %collective-permute-start.14 = (bf16[160,384]{1,0:T(8,128)(2,1)S(1)}, bf16[160,384]{1,0:T(8,128)(2,1)S(1)}, u32[]{:S(2)}, u32[]{:S(2)}) collective-permute-start(bf16[160,384]{1,0:T(8,128)(2,1)S(1)} %slice.192), channel_id=1, source_target_pairs={{0,2},{2,4},{4,6},{6,0},{1,3},{3,5},{5,7},{7,1},{8,10},{10,12},{12... | collective-permute-start | bytes 368648 | tf_op jit(solution)/shard_map/ppermute | solution.py:33
  73.5 6.7 %collective-permute-start.19 = (bf16[160,768]{1,0:T(8,128)(2,1)S(1)}, bf16[160,768]{1,0:T(8,128)(2,1)S(1)}, u32[]{:S(2)}, u32[]{:S(2)}) collective-permute-start(bf16[160,768]{1,0:T(8,128)(2,1)S(1)} %pad_maximum_fusion.6), channel_id=1, source_target_pairs={{0,24},{8,0},{16,8},{24,16},{1,25},{9,1},{17,9},{25,17},{2,26},{10... | collective-permute-start | bytes 737288 | tf_op jit(solution)/shard_map/ppermute | solution.py:33
  76.4 7.4 %collective-permute-start.18 = (bf16[160,768]{1,0:T(8,128)(2,1)S(1)}, bf16[160,768]{1,0:T(8,128)(2,1)S(1)}, u32[]{:S(2)}, u32[]{:S(2)}) collective-permute-start(bf16[160,768]{1,0:T(8,128)(2,1)S(1)} %pad_maximum_fusion.6), channel_id=1, source_target_pairs={{0,8},{8,16},{16,24},{24,0},{1,9},{9,17},{17,25},{25,1},{2,10},{10... | collective-permute-start | bytes 737288 | tf_op jit(solution)/shard_map/ppermute | solution.py:33
  83.9 13.8 %collective-permute-start.21 = (bf16[160,1536]{1,0:T(8,128)(2,1)S(1)}, bf16[160,1536]{1,0:T(8,128)(2,1)S(1)}, u32[]{:S(2)}, u32[]{:S(2)}) collective-permute-start(bf16[160,1536]{1,0:T(8,128)(2,1)S(1)} %slice.195), channel_id=1, source_target_pairs={{0,24},{8,0},{16,8},{24,16},{1,25},{9,1},{17,9},{25,17},{2,26},{10... | collective-permute-start | bytes 1474568 | tf_op jit(solution)/shard_map/ppermute | solution.py:33
  84.0 14.5 %collective-permute-start.20 = (bf16[160,1536]{1,0:T(8,128)(2,1)S(1)}, bf16[160,1536]{1,0:T(8,128)(2,1)}, u32[]{:S(2)}, u32[]{:S(2)}) collective-permute-start(bf16[160,1536]{1,0:T(8,128)(2,1)S(1)} %slice.194), channel_id=1, source_target_pairs={{0,8},{8,16},{16,24},{24,0},{1,9},{9,17},{17,25},{25,1},{2,10},{10... | collective-permute-start | bytes 1474568 | tf_op jit(solution)/shard_map/ppermute | solution.py:33
  86.1 10.3 %collective-permute-start.23 = (bf16[160,384]{1,0:T(8,128)(2,1)S(1)}, bf16[160,384]{1,0:T(8,128)(2,1)S(1)}, u32[]{:S(2)}, u32[]{:S(2)}) collective-permute-start(bf16[160,384]{1,0:T(8,128)(2,1)S(1)} %slice.197), channel_id=1, source_target_pairs={{0,24},{8,0},{16,8},{24,16},{1,25},{9,1},{17,9},{25,17},{2,26},{10... | collective-permute-start | bytes 368648 | tf_op jit(solution)/shard_map/ppermute | solution.py:33
  87.4 10.3 %collective-permute-start.22 = (bf16[160,384]{1,0:T(8,128)(2,1)S(1)}, bf16[160,384]{1,0:T(8,128)(2,1)S(1)}, u32[]{:S(2)}, u32[]{:S(2)}) collective-permute-start(bf16[160,384]{1,0:T(8,128)(2,1)S(1)} %slice.196), channel_id=1, source_target_pairs={{0,8},{8,16},{16,24},{24,0},{1,9},{9,17},{17,25},{25,1},{2,10},{10... | collective-permute-start | bytes 368648 | tf_op jit(solution)/shard_map/ppermute | solution.py:33
  99.5 126.7 %reduce-scatter.3.cloned.1.call-start = ((), (), s32[]{:S(2)}) async-start(), calls=%async_computation.2 | async-start | bytes 8847360 | tf_op jit(solution)/shard_map/reduce_scatter | solution.py:449
  99.6 2.2 collective-permute-start.29
  99.6 3.6 %collective-permute-start.30 = (bf16[160,1536]{1,0:T(8,128)(2,1)}, bf16[160,1536]{1,0:T(8,128)(2,1)}, u32[]{:S(2)}, u32[]{:S(2)}) collective-permute-start(bf16[160,1536]{1,0:T(8,128)(2,1)} %copy-done.11), channel_id=1, source_target_pairs={{0,1},{1,0},{2,3},{3,2},{4,5},{5,4},{6,7},{7,6},{8,9},{9,8},{10,11... | collective-permute-start | bytes 1474568 | tf_op jit(solution)/shard_map/ppermute | solution.py:41
  100.1 4.5 %collective-permute-start.27 = (bf16[160,3072]{1,0:T(8,128)(2,1)S(1)}, bf16[160,3072]{1,0:T(8,128)(2,1)}, u32[]{:S(2)}, u32[]{:S(2)}) collective-permute-start(bf16[160,3072]{1,0:T(8,128)(2,1)S(1)} %collective-permute-done.16.refs_1_), channel_id=1, source_target_pairs={{0,1},{1,0},{2,3},{3,2},{4,5},{5,4},{6,7},{7,6},{8,9},{9,8},{10,11... | collective-permute-start | bytes 2949128 | tf_op jit(solution)/shard_map/ppermute | solution.py:41
  100.2 6.3 %collective-permute-start.28 = (bf16[160,3072]{1,0:T(8,128)(2,1)S(1)}, bf16[160,3072]{1,0:T(8,128)(2,1)}, u32[]{:S(2)}, u32[]{:S(2)}) collective-permute-start(bf16[160,3072]{1,0:T(8,128)(2,1)S(1)} %collective-permute-done.17.refs_2_), channel_id=1, source_target_pairs={{0,1},{1,0},{2,3},{3,2},{4,5},{5,4},{6,7},{7,6},{8,9},{9,8},{10,11... | collective-permute-start | bytes 2949128 | tf_op jit(solution)/shard_map/ppermute | solution.py:41
  100.9 17.2 %collective-permute-start.26 = (bf16[160,3072]{1,0:T(8,128)(2,1)}, bf16[160,3072]{1,0:T(8,128)(2,1)}, u32[]{:S(2)}, u32[]{:S(2)}) collective-permute-start(bf16[160,3072]{1,0:T(8,128)(2,1)} %copy-done.6), channel_id=1, source_target_pairs={{0,1},{1,0},{2,3},{3,2},{4,5},{5,4},{6,7},{7,6},{8,9},{9,8},{10,11... | collective-permute-start | bytes 2949128 | tf_op jit(solution)/shard_map/ppermute | solution.py:41
  101.7 24.1 %collective-permute-start.25 = (bf16[160,3072]{1,0:T(8,128)(2,1)}, bf16[160,3072]{1,0:T(8,128)(2,1)}, u32[]{:S(2)}, u32[]{:S(2)}) collective-permute-start(bf16[160,3072]{1,0:T(8,128)(2,1)} %copy-done.6), channel_id=1, source_target_pairs={{0,24},{8,0},{16,8},{24,16},{1,25},{9,1},{17,9},{25,17},{2,26},{10... | collective-permute-start | bytes 2949128 | tf_op jit(solution)/shard_map/ppermute | solution.py:33
  103.2 25.3 %collective-permute-start.24 = (bf16[160,3072]{1,0:T(8,128)(2,1)}, bf16[160,3072]{1,0:T(8,128)(2,1)}, u32[]{:S(2)}, u32[]{:S(2)}) collective-permute-start(bf16[160,3072]{1,0:T(8,128)(2,1)} %copy-done.6), channel_id=1, source_target_pairs={{0,8},{8,16},{16,24},{24,0},{1,9},{9,17},{17,25},{25,1},{2,10},{10... | collective-permute-start | bytes 2949128 | tf_op jit(solution)/shard_map/ppermute | solution.py:33
  128.6 21.4 %collective-permute-start.33 = (bf16[160,3072]{1,0:T(8,128)(2,1)}, bf16[160,3072]{1,0:T(8,128)(2,1)S(1)}, u32[]{:S(2)}, u32[]{:S(2)}) collective-permute-start(bf16[160,3072]{1,0:T(8,128)(2,1)} %collective-permute-done.24.refs_1_), channel_id=1, source_target_pairs={{0,1},{1,0},{2,3},{3,2},{4,5},{5,4},{6,7},{7,6},{8,9},{9,8},{10,11... | collective-permute-start | bytes 2949128 | tf_op jit(solution)/shard_map/ppermute | solution.py:41
  128.6 21.4 %collective-permute-start.34 = (bf16[160,3072]{1,0:T(8,128)(2,1)}, bf16[160,3072]{1,0:T(8,128)(2,1)}, u32[]{:S(2)}, u32[]{:S(2)}) collective-permute-start(bf16[160,3072]{1,0:T(8,128)(2,1)} %collective-permute-done.25.refs_2_), channel_id=1, source_target_pairs={{0,1},{1,0},{2,3},{3,2},{4,5},{5,4},{6,7},{7,6},{8,9},{9,8},{10,11... | collective-permute-start | bytes 2949128 | tf_op jit(solution)/shard_map/ppermute | solution.py:41
  131.2 18.7 %collective-permute-start.32 = (bf16[160,1536]{1,0:T(8,128)(2,1)S(1)}, bf16[160,1536]{1,0:T(8,128)(2,1)S(1)}, u32[]{:S(2)}, u32[]{:S(2)}) collective-permute-start(bf16[160,1536]{1,0:T(8,128)(2,1)S(1)} %slice.199), channel_id=1, source_target_pairs={{0,24},{8,0},{16,8},{24,16},{1,25},{9,1},{17,9},{25,17},{2,26},{10... | collective-permute-start | bytes 1474568 | tf_op jit(solution)/shard_map/ppermute | solution.py:33
  131.3 18.7 %collective-permute-start.31 = (bf16[160,1536]{1,0:T(8,128)(2,1)S(1)}, bf16[160,1536]{1,0:T(8,128)(2,1)}, u32[]{:S(2)}, u32[]{:S(2)}) collective-permute-start(bf16[160,1536]{1,0:T(8,128)(2,1)S(1)} %slice.198), channel_id=1, source_target_pairs={{0,8},{8,16},{16,24},{24,0},{1,9},{9,17},{17,25},{25,1},{2,10},{10... | collective-permute-start | bytes 1474568 | tf_op jit(solution)/shard_map/ppermute | solution.py:33
  151.0 109.5 %reduce-scatter.5.cloned.1.call-start = ((), (), s32[]{:S(2)}) async-start(), calls=%async_computation.3 | async-start | bytes 1228800 | tf_op jit(solution)/shard_map/reduce_scatter | solution.py:450
  151.0 10.6 %collective-permute-start.35 = (bf16[160,1536]{1,0:T(8,128)(2,1)}, bf16[160,1536]{1,0:T(8,128)(2,1)S(1)}, u32[]{:S(2)}, u32[]{:S(2)}) collective-permute-start(bf16[160,1536]{1,0:T(8,128)(2,1)} %collective-permute-done.31.refs_3_), channel_id=1, source_target_pairs={{0,1},{1,0},{2,3},{3,2},{4,5},{5,4},{6,7},{7,6},{8,9},{9,8},{10,11... | collective-permute-start | bytes 1474568 | tf_op jit(solution)/shard_map/ppermute | solution.py:41
  159.6 2.5 collective-permute-start.36
  190.6 9.4 %collective-permute-start.37 = (bf16[640,3072]{1,0:T(8,128)(2,1)}, bf16[640,3072]{1,0:T(8,128)(2,1)}, u32[]{:S(2)}, u32[]{:S(2)}) collective-permute-start(bf16[640,3072]{1,0:T(8,128)(2,1)} %get-tuple-element.110), channel_id=1, source_target_pairs={{0,1},{1,0},{2,3},{3,2},{4,5},{5,4},{6,7},{7,6},{8,9},{9,8},{10,11... | collective-permute-start | bytes 11796488 | tf_op jit(solution)/shard_map/ppermute | solution.py:41
  201.2 14.8 %collective-permute-start.41 = (bf16[320,384]{1,0:T(8,128)(2,1)S(1)}, bf16[320,384]{1,0:T(8,128)(2,1)S(1)}, u32[]{:S(2)}, u32[]{:S(2)}) collective-permute-start(bf16[320,384]{1,0:T(8,128)(2,1)S(1)} %get-tuple-element.145), channel_id=1, source_target_pairs={{0,6},{2,0},{4,2},{6,4},{1,7},{3,1},{5,3},{7,5},{8,14},{10,8},{12,... | collective-permute-start | bytes 737288 | tf_op jit(solution)/shard_map/ppermute | solution.py:33
  203.4 12.7 %collective-permute-start.40 = (bf16[320,384]{1,0:T(8,128)(2,1)S(1)}, bf16[320,384]{1,0:T(8,128)(2,1)S(1)}, u32[]{:S(2)}, u32[]{:S(2)}) collective-permute-start(bf16[320,384]{1,0:T(8,128)(2,1)S(1)} %get-tuple-element.146), channel_id=1, source_target_pairs={{0,2},{2,4},{4,6},{6,0},{1,3},{3,5},{5,7},{7,1},{8,10},{10,12},{12... | collective-permute-start | bytes 737288 | tf_op jit(solution)/shard_map/ppermute | solution.py:33
  204.6 11.5 %collective-permute-start.39 = (bf16[160,768]{1,0:T(8,128)(2,1)S(1)}, bf16[160,768]{1,0:T(8,128)(2,1)S(1)}, u32[]{:S(2)}, u32[]{:S(2)}) collective-permute-start(bf16[160,768]{1,0:T(8,128)(2,1)S(1)} %get-tuple-element.147), channel_id=1, source_target_pairs={{0,24},{8,0},{16,8},{24,16},{1,25},{9,1},{17,9},{25,17},{2,26},{10... | collective-permute-start | bytes 737288 | tf_op jit(solution)/shard_map/ppermute | solution.py:33
  207.1 8.9 %collective-permute-start.38 = (bf16[160,768]{1,0:T(8,128)(2,1)S(1)}, bf16[160,768]{1,0:T(8,128)(2,1)S(1)}, u32[]{:S(2)}, u32[]{:S(2)}) collective-permute-start(bf16[160,768]{1,0:T(8,128)(2,1)S(1)} %get-tuple-element.148), channel_id=1, source_target_pairs={{0,8},{8,16},{16,24},{24,0},{1,9},{9,17},{17,25},{25,1},{2,10},{10... | collective-permute-start | bytes 737288 | tf_op jit(solution)/shard_map/ppermute | solution.py:33
  218.4 24.2 %collective-permute-start.43 = (bf16[160,1536]{1,0:T(8,128)(2,1)}, bf16[160,1536]{1,0:T(8,128)(2,1)S(1)}, u32[]{:S(2)}, u32[]{:S(2)}) collective-permute-start(bf16[160,1536]{1,0:T(8,128)(2,1)} %get-tuple-element.137), channel_id=1, source_target_pairs={{0,24},{8,0},{16,8},{24,16},{1,25},{9,1},{17,9},{25,17},{2,26},{10... | collective-permute-start | bytes 1474568 | tf_op jit(solution)/shard_map/ppermute | solution.py:33
  221.6 20.9 %collective-permute-start.42 = (bf16[160,1536]{1,0:T(8,128)(2,1)S(1)}, bf16[160,1536]{1,0:T(8,128)(2,1)S(1)}, u32[]{:S(2)}, u32[]{:S(2)}) collective-permute-start(bf16[160,1536]{1,0:T(8,128)(2,1)S(1)} %get-tuple-element.138), channel_id=1, source_target_pairs={{0,8},{8,16},{16,24},{24,0},{1,9},{9,17},{17,25},{25,1},{2,10},{10... | collective-permute-start | bytes 1474568 | tf_op jit(solution)/shard_map/ppermute | solution.py:33
  224.1 18.4 %collective-permute-start.45 = (bf16[640,384]{1,0:T(8,128)(2,1)}, bf16[640,384]{1,0:T(8,128)(2,1)S(1)}, u32[]{:S(2)}, u32[]{:S(2)}) collective-permute-start(bf16[640,384]{1,0:T(8,128)(2,1)} %get-tuple-element.135), channel_id=1, source_target_pairs={{0,6},{2,0},{4,2},{6,4},{1,7},{3,1},{5,3},{7,5},{8,14},{10,8},{12,... | collective-permute-start | bytes 1474568 | tf_op jit(solution)/shard_map/ppermute | solution.py:33
  225.9 16.7 %collective-permute-start.44 = (bf16[640,384]{1,0:T(8,128)(2,1)}, bf16[640,384]{1,0:T(8,128)(2,1)S(1)}, u32[]{:S(2)}, u32[]{:S(2)}) collective-permute-start(bf16[640,384]{1,0:T(8,128)(2,1)} %get-tuple-element.136), channel_id=1, source_target_pairs={{0,2},{2,4},{4,6},{6,0},{1,3},{3,5},{5,7},{7,1},{8,10},{10,12},{12... | collective-permute-start | bytes 1474568 | tf_op jit(solution)/shard_map/ppermute | solution.py:33
  244.1 8.9 %collective-permute-start.49 = (bf16[160,384]{1,0:T(8,128)(2,1)S(1)}, bf16[160,384]{1,0:T(8,128)(2,1)S(1)}, u32[]{:S(2)}, u32[]{:S(2)}) collective-permute-start(bf16[160,384]{1,0:T(8,128)(2,1)S(1)} %get-tuple-element.142), channel_id=1, source_target_pairs={{0,24},{8,0},{16,8},{24,16},{1,25},{9,1},{17,9},{25,17},{2,26},{10... | collective-permute-start | bytes 368648 | tf_op jit(solution)/shard_map/ppermute | solution.py:33
  247.4 6.9 %collective-permute-start.51 = (bf16[160,384]{1,0:T(8,128)(2,1)S(1)}, bf16[160,384]{1,0:T(8,128)(2,1)S(1)}, u32[]{:S(2)}, u32[]{:S(2)}) collective-permute-start(bf16[160,384]{1,0:T(8,128)(2,1)S(1)} %get-tuple-element.143), channel_id=1, source_target_pairs={{0,16},{8,24},{16,0},{24,8},{1,17},{9,25},{17,1},{25,9},{2,18},{10... | collective-permute-start | bytes 368648 | tf_op jit(solution)/shard_map/ppermute | solution.py:33
  247.4 7.5 %collective-permute-start.50 = (bf16[160,384]{1,0:T(8,128)(2,1)S(1)}, bf16[160,384]{1,0:T(8,128)(2,1)S(1)}, u32[]{:S(2)}, u32[]{:S(2)}) collective-permute-start(bf16[160,384]{1,0:T(8,128)(2,1)S(1)} %get-tuple-element.144), channel_id=1, source_target_pairs={{0,8},{8,16},{16,24},{24,0},{1,9},{9,17},{17,25},{25,1},{2,10},{10... | collective-permute-start | bytes 368648 | tf_op jit(solution)/shard_map/ppermute | solution.py:33
  249.9 5.2 %collective-permute-start.46 = (bf16[160,384]{1,0:T(8,128)(2,1)S(1)}, bf16[160,384]{1,0:T(8,128)(2,1)S(1)}, u32[]{:S(2)}, u32[]{:S(2)}) collective-permute-start(bf16[160,384]{1,0:T(8,128)(2,1)S(1)} %get-tuple-element.139), channel_id=1, source_target_pairs={{0,6},{2,0},{4,2},{6,4},{1,7},{3,1},{5,3},{7,5},{8,14},{10,8},{12,... | collective-permute-start | bytes 368648 | tf_op jit(solution)/shard_map/ppermute | solution.py:33
  252.7 6.5 %collective-permute-start.48 = (bf16[160,384]{1,0:T(8,128)(2,1)S(1)}, bf16[160,384]{1,0:T(8,128)(2,1)S(1)}, u32[]{:S(2)}, u32[]{:S(2)}) collective-permute-start(bf16[160,384]{1,0:T(8,128)(2,1)S(1)} %get-tuple-element.140), channel_id=1, source_target_pairs={{0,4},{2,6},{4,0},{6,2},{1,5},{3,7},{5,1},{7,3},{8,12},{10,14},{12... | collective-permute-start | bytes 368648 | tf_op jit(solution)/shard_map/ppermute | solution.py:33
  253.0 7.4 %collective-permute-start.47 = (bf16[160,384]{1,0:T(8,128)(2,1)S(1)}, bf16[160,384]{1,0:T(8,128)(2,1)S(1)}, u32[]{:S(2)}, u32[]{:S(2)}) collective-permute-start(bf16[160,384]{1,0:T(8,128)(2,1)S(1)} %get-tuple-element.141), channel_id=1, source_target_pairs={{0,2},{2,4},{4,6},{6,0},{1,3},{3,5},{5,7},{7,1},{8,10},{10,12},{12... | collective-permute-start | bytes 368648 | tf_op jit(solution)/shard_map/ppermute | solution.py:33
  261.5 5.3 %collective-permute-start.52 = (bf16[80,768]{1,0:T(8,128)(2,1)S(1)}, bf16[80,768]{1,0:T(8,128)(2,1)S(1)}, u32[]{:S(2)}, u32[]{:S(2)}) collective-permute-start(bf16[80,768]{1,0:T(8,128)(2,1)S(1)} %get-tuple-element.159), channel_id=1, source_target_pairs={{0,96},{32,0},{64,32},{96,64},{1,97},{33,1},{65,33},{97,65},{2,98}... | collective-permute-start | bytes 368648 | tf_op jit(solution)/shard_map/ppermute | solution.py:33
  264.3 6.6 %collective-permute-start.53 = (bf16[80,768]{1,0:T(8,128)(2,1)S(1)}, bf16[80,768]{1,0:T(8,128)(2,1)S(1)}, u32[]{:S(2)}, u32[]{:S(2)}) collective-permute-start(bf16[80,768]{1,0:T(8,128)(2,1)S(1)} %get-tuple-element.160), channel_id=1, source_target_pairs={{0,64},{32,96},{64,0},{96,32},{1,65},{33,97},{65,1},{97,33},{2,66}... | collective-permute-start | bytes 368648 | tf_op jit(solution)/shard_map/ppermute | solution.py:33
  264.7 7.4 %collective-permute-start.54 = (bf16[80,768]{1,0:T(8,128)(2,1)S(1)}, bf16[80,768]{1,0:T(8,128)(2,1)S(1)}, u32[]{:S(2)}, u32[]{:S(2)}) collective-permute-start(bf16[80,768]{1,0:T(8,128)(2,1)S(1)} %get-tuple-element.161), channel_id=1, source_target_pairs={{0,32},{32,64},{64,96},{96,0},{1,33},{33,65},{65,97},{97,1},{2,34}... | collective-permute-start | bytes 368648 | tf_op jit(solution)/shard_map/ppermute | solution.py:33
  272.7 1.2 collective-permute-start.55
  273.8 4.0 %collective-permute-start.58 = (f32[128,2]{0,1:T(2,128)S(1)}, f32[128,2]{0,1:T(2,128)S(1)}, u32[]{:S(2)}, u32[]{:S(2)}) collective-permute-start(f32[128,2]{0,1:T(2,128)S(1)} %add.237), channel_id=1, source_target_pairs={{0,6},{2,0},{4,2},{6,4},{1,7},{3,1},{5,3},{7,5},{8,14},{10,8},{12,... | collective-permute-start | bytes 3080 | tf_op jit(solution)/shard_map/ppermute | solution.py:33
  274.7 4.8 %collective-permute-start.57 = (f32[128,2]{0,1:T(2,128)S(1)}, f32[128,2]{0,1:T(2,128)S(1)}, u32[]{:S(2)}, u32[]{:S(2)}) collective-permute-start(f32[128,2]{0,1:T(2,128)S(1)} %add.237), channel_id=1, source_target_pairs={{0,2},{2,4},{4,6},{6,0},{1,3},{3,5},{5,7},{7,1},{8,10},{10,12},{12... | collective-permute-start | bytes 3080 | tf_op jit(solution)/shard_map/ppermute | solution.py:33
  275.8 5.1 %collective-permute-start.56 = (f32[128,2]{0,1:T(2,128)S(1)}, f32[128,2]{0,1:T(2,128)S(1)}, u32[]{:S(2)}, u32[]{:S(2)}) collective-permute-start(f32[128,2]{0,1:T(2,128)S(1)} %add.237), channel_id=1, source_target_pairs={{0,4},{2,6},{4,0},{6,2},{1,5},{3,7},{5,1},{7,3},{8,12},{10,14},{12... | collective-permute-start | bytes 3080 | tf_op jit(solution)/shard_map/ppermute | solution.py:33
  (15 other events, 206.6 us)
Sparse Core Ops, SparseCore 0:
  46.4 51.2 all-gather.6
  99.6 46.8 all-gather.4
  150.2 49.9 reduce-scatter.2
  226.3 26.3 reduce-scatter.4
